TPU v7x, 32 devices: a whole 2x2x4 slice. The times are simulated.
32 devices in a mesh: dp: 8 (over z, y), fsdp: 4 (over x, core).
Axes of the slice: x: 2, y: 2, z: 4, core: 2. Of those that a mesh axis runs over, the one named last changes fastest.
Arguments:
- tokens: bfloat16 [8192, 2048], P(('dp', 'fsdp')), may hold values from -6 to 6
- widths: int32 [8], P('dp'), may hold values from 0 to 3, as said below
- cotangent: bfloat16 [8192, 2048], P(('dp', 'fsdp')), may hold values from -6 to 6
- in_weight: float32 [2048, 8512], P(('dp', 'fsdp')), may hold values from -0.125 to 0.125
- in_first: float32 [2048, 8512], P(('dp', 'fsdp')), may hold values from -0.0029296875 to 0.0029296875
- in_second: float32 [2048, 8512], P(('dp', 'fsdp')), may hold values from 3.8685798e-08 to 1.5474319e-07
- out_weight: float32 [4096, 2048], P(('dp', 'fsdp')), may hold values from -0.09375 to 0.09375
- out_first: float32 [4096, 2048], P(('dp', 'fsdp')), may hold values from -0.0029296875 to 0.0029296875
- out_second: float32 [4096, 2048], P(('dp', 'fsdp')), may hold values from 3.8685798e-08 to 1.5474319e-07
- vectors: float32 [28096], replicated, may hold values from -8 to 3
- vector_first: float32 [28096], replicated, may hold values from -0.0078125 to 0.0078125
- vector_second: float32 [28096], replicated, may hold values from 1.5474319e-07 to 6.1897276e-07
Outputs:
- layer_out: bfloat16 [8192, 2048], P(('dp', 'fsdp'))
- token_grad: bfloat16 [8192, 2048], P(('dp', 'fsdp'))
- in_grad: float32 [2048, 8512], P(('dp', 'fsdp'))
- out_grad: float32 [4096, 2048], P(('dp', 'fsdp'))
- vector_grad: float32 [28096], replicated
- grad_norm: float32 [], replicated
- in_moment: float32 [2048, 8512], P(('dp', 'fsdp'))
- in_square: float32 [2048, 8512], P(('dp', 'fsdp'))
- in_master: float32 [2048, 8512], P(('dp', 'fsdp'))
- in_rounded: bfloat16 [2048, 8512], P(('dp', 'fsdp'))
- out_moment: float32 [4096, 2048], P(('dp', 'fsdp'))
- out_square: float32 [4096, 2048], P(('dp', 'fsdp'))
- out_master: float32 [4096, 2048], P(('dp', 'fsdp'))
- out_rounded: bfloat16 [4096, 2048], P(('dp', 'fsdp'))
- vector_moment: float32 [28096], replicated
- vector_square: float32 [28096], replicated
- vector_master: float32 [28096], replicated
Inputs may be any that keep to these rules, and one draw needn't show every extreme that they name: `widths`: every width index 0, 1, 2 and 3 occurs in every draw.
All inputs are finite; a program needn't handle non-finite values.
Results may differ from a plain program's by a relative error of at most 0.0087.
The roundings to bfloat16 on the way count: a program that leaves them out, or rounds other values in their place, can miss the bound.
Values may be sent and summed in bfloat16 or wider, within the bound.
A program may use at most 232 MiB of HBM per device.

v0:
```python
from functools import partial

import jax
import jax.numpy as jnp
import numpy as np
from jax import lax
from jax.experimental import pallas as pl
from jax.experimental.pallas import tpu as pltpu
from jax.sharding import PartitionSpec as P

D = 2048
HEADS = 64
HEAD_DIM = 64
STATE = 128
CONV = 4
SPAN = 128
STEP = 10
INNER = 4096
XBC = 4352
PAIR = 2 * HEAD_DIM
GROUP = 4
STEP_LANE = 16
TAPS_ROW = (D + INNER) // PAIR
LAST_ROW = TAPS_ROW + (CONV + 1) * XBC // PAIR
MASK_ROW, SKIP_ROW, GAIN_ROW = CONV + 1, CONV + 2, CONV + 3
LANES = GROUP * HEAD_DIM
ROW_TILE = 256
RING_LIMIT = 16

norm_eps = 1e-05
clip_norm = 1.0
beta_first = 0.5
beta_second = 0.5
adam_eps = 1e-08
weight_decay = 0.1
rate_in_proj = 0.03
rate_out_proj = 0.02
rate_vectors = 0.5
highest = lax.Precision.HIGHEST
f32 = jnp.float32
bf16 = jnp.bfloat16
VMEM_BYTES = 60 * 1024 * 1024
BACKWARD_VMEM_BYTES = 63 * 1024 * 1024


def ring_order(count):
    return list(range(0, count, 2)) + list(range(count - 1, 0, -2))


def ring_links(count):
    order = ring_order(count)
    right = [(order[i], order[(i + 1) % count]) for i in range(count)]
    return right, [(b, a) for a, b in right]


def ring_place(axis):
    count = lax.axis_size(axis)
    order = ring_order(count)
    places = [0] * count
    for place, member in enumerate(order):
        places[member] = place
    place = jnp.asarray(places, jnp.int32)[lax.axis_index(axis)]

    def member_at(distance):
        return jnp.asarray(order, jnp.int32)[lax.rem(place + distance + count, count)]

    return member_at


def uses_ring(axis):
    count = lax.axis_size(axis)
    return count % 2 == 0 and 4 <= count <= RING_LIMIT


def gather_rows(block, axis):
    count = lax.axis_size(axis)
    if not uses_ring(axis):
        return lax.all_gather(block, axis, axis=0, tiled=True)
    right, left = ring_links(count)
    member_at = ring_place(axis)
    rows, half = block.shape[0], block.shape[0] // 2
    whole = jnp.zeros((count * rows,) + block.shape[1:], block.dtype)
    columns = (0,) * (block.ndim - 1)

    def put(whole, piece, distance, shift=0):
        return lax.dynamic_update_slice(
            whole, piece, (member_at(distance) * rows + shift,) + columns
        )

    whole = put(whole, block, 0)
    going_right = going_left = block
    for hop in range(1, count // 2):
        going_right = lax.ppermute(going_right, axis, right)
        going_left = lax.ppermute(going_left, axis, left)
        whole = put(whole, going_right, -hop)
        whole = put(whole, going_left, hop)
    first = lax.ppermute(going_right[:half], axis, right)
    second = lax.ppermute(going_left[half:], axis, left)
    whole = put(whole, first, count // 2)
    return put(whole, second, count // 2, half)


def scatter_rows(terms, axis):
    count = lax.axis_size(axis)
    if not uses_ring(axis):
        return lax.psum_scatter(terms.astype(f32), axis, scatter_dimension=0, tiled=True)
    right, left = ring_links(count)
    member_at = ring_place(axis)
    rows = terms.shape[0] // count
    half = rows // 2

    def term(distance):
        return lax.dynamic_slice_in_dim(terms, member_at(distance) * rows, rows, 0).astype(f32)

    far = term(count // 2).astype(bf16)
    going_right = lax.ppermute(far[:half], axis, right)
    going_left = lax.ppermute(far[half:], axis, left)
    for distance in range(count // 2 - 1, 0, -1):
        to_right, to_left = term(distance), term(-distance)
        if distance == count // 2 - 1:
            to_right = jnp.concatenate([to_right[:half] + going_right, to_right[half:]])
            to_left = jnp.concatenate([to_left[:half], to_left[half:] + going_left])
        else:
            to_right, to_left = to_right + going_right, to_left + going_left
        going_right = lax.ppermute(to_right.astype(bf16), axis, right)
        going_left = lax.ppermute(to_left.astype(bf16), axis, left)
    return term(0) + going_right + going_left


def swapped(value, axis, flip):
    count = lax.axis_size(axis)
    return lax.ppermute(value, axis, [(i, i ^ flip) for i in range(count)])


def summed(value, axis):
    count = lax.axis_size(axis)
    if count <= 8:
        parts = [value] + [swapped(value, axis, flip) for flip in range(1, count)]
        while len(parts) > 1:
            parts = [parts[i] + parts[i + 1] for i in range(0, len(parts), 2)]
        return parts[0]
    return summed_in_steps(value, axis)


def summed_in_steps(value, axis):
    flip = 1
    while flip < lax.axis_size(axis):
        value = value + swapped(value, axis, flip)
        flip *= 2
    return value


def placed(parts, axis):
    count = lax.axis_size(axis)
    me = lax.axis_index(axis)
    whole = jnp.zeros((count,) + parts[0].shape, parts[0].dtype)
    for flip, part in enumerate(parts):
        whole = lax.dynamic_update_index_in_dim(whole, part, lax.bitwise_xor(me, flip), 0)
    return whole


def spread(value, axis):
    count = lax.axis_size(axis)
    parts = [value]
    flip = count // 2
    known = {0: value}
    while flip:
        fresh = {k ^ flip: swapped(v, axis, flip) for k, v in known.items()}
        known.update(fresh)
        flip //= 2
    parts = [known[k] for k in range(count)]
    return placed(parts, axis)


def spread_small(value, axis):
    count = lax.axis_size(axis)
    return placed([value] + [swapped(value, axis, k) for k in range(1, count)], axis)


def exchanged(blocks, axis):
    count = lax.axis_size(axis)
    me = lax.axis_index(axis)

    def block_for(flip):
        return lax.dynamic_index_in_dim(blocks, lax.bitwise_xor(me, flip), 0, False)

    return placed(
        [block_for(0)] + [swapped(block_for(k), axis, k) for k in range(1, count)], axis
    )


def halved(blocks, axis):
    count = lax.axis_size(axis)
    me = lax.axis_index(axis)
    held = {
        k: lax.dynamic_index_in_dim(blocks, lax.bitwise_xor(me, k), 0, False)
        for k in range(count)
    }
    flip = 1
    while flip < count:
        kept = {}
        for k in sorted(held):
            if k & flip:
                continue
            arrived = swapped(held[k ^ flip].astype(bf16), axis, flip)
            kept[k] = held[k].astype(f32) + arrived
        held = kept
        flip *= 2
    return held[0]


def dot_rows(a, b):
    return lax.dot_general(a, b, (((1,), (0,)), ((), ())), preferred_element_type=f32)


def dot_lanes(a, b):
    return lax.dot_general(a, b, (((1,), (1,)), ((), ())), preferred_element_type=f32)


def head_lanes(columns, base):
    rows = columns.shape[0]
    full = [
        jnp.broadcast_to(columns[:, base + j : base + j + 1], (rows, PAIR)) for j in range(GROUP)
    ]
    first = lax.broadcasted_iota(jnp.int32, (rows, PAIR), 1) < HEAD_DIM
    lanes = jnp.concatenate(
        [jnp.where(first, full[i], full[i + 1]) for i in range(0, GROUP, 2)], axis=1
    )
    return full, lanes


def stacked_heads(values, block_mask):
    return jnp.concatenate([values] * GROUP, axis=0) * block_mask


def filtered(window, taps, bias, rows):
    pre = bias + taps[CONV - 1 : CONV] * window[8 : 8 + rows]
    for k in range(CONV - 1):
        pre = pre + taps[k : k + 1] * window[5 + k : 5 + k + rows]
    return pre


def scan_forward_kernel(
    x_ref, consts_ref, column_ref, row_ref, key_ref, query_ref,
    key_t_ref, block_ref, y_ref, states_ref, padded, state,
):
    length = x_ref.shape[0]
    rows = SPAN
    mask = consts_ref[MASK_ROW : MASK_ROW + 1]
    padded[0:8, :] = jnp.zeros((8, LANES), f32)
    padded[8 : 8 + length, :] = x_ref[...] * mask
    state[...] = jnp.zeros_like(state)
    taps, bias = consts_ref[0:CONV], consts_ref[CONV : CONV + 1]
    skip = consts_ref[SKIP_ROW : SKIP_ROW + 1]
    causal = lax.broadcasted_iota(jnp.int32, (rows, rows), 0) >= lax.broadcasted_iota(
        jnp.int32, (rows, rows), 1
    )

    def chunk(c, carry):
        start = pl.multiple_of(c * rows, rows)
        here = pl.ds(start, rows)
        pre = filtered(padded[pl.ds(start, rows + 8), :], taps, bias, rows)
        values = pre * jax.nn.sigmoid(pre) * mask
        columns = column_ref[here, :]
        log_full, log_lanes = head_lanes(columns, 0)
        step_lanes = head_lanes(columns, STEP_LANE)[1]
        weighted = step_lanes * values
        weighted_low = weighted.astype(bf16)
        keys, queries, keys_t = key_ref[here, :], query_ref[here, :], key_t_ref[:, here]
        inner = dot_lanes(queries, keys)
        mixing = jnp.concatenate(
            [
                (
                    jnp.where(causal, jnp.exp(log_full[j] - row_ref[j : j + 1, here]), 0.0)
                    * inner
                ).astype(bf16)
                for j in range(GROUP)
            ],
            axis=1,
        )
        state_now = state[...]
        state_low = state_now.astype(bf16)
        states_ref[pl.ds(c, 1)] = state_low[None]
        y = dot_rows(mixing, stacked_heads(weighted_low, block_ref[...]))
        y = y + jnp.exp(log_lanes) * dot_rows(queries, state_low)
        y_ref[here, :] = y + skip * values
        log_last = log_lanes[rows - 1 : rows, :]
        tail = (weighted * jnp.exp(log_last - log_lanes)).astype(bf16)
        state[...] = jnp.exp(log_last) * state_now + dot_rows(keys_t, tail)
        return carry

    lax.fori_loop(0, length // rows, chunk, 0)


def scan_backward_group(
    x_ref, consts_ref, column_ref, row_ref, key_ref, query_ref,
    query_t_ref, block_ref, pick_ref, grad_ref, states_ref,
    x_grad_ref, key_grad_ref, query_grad_ref, sums_ref, rest_ref, channel_ref,
    padded, following, state_back, inner_grad,
):
    length = x_ref.shape[0]
    rows = SPAN
    chunks = length // rows
    mask = consts_ref[MASK_ROW : MASK_ROW + 1]
    padded[0:8, :] = jnp.zeros((8, LANES), f32)
    padded[8 : 8 + length, :] = x_ref[...] * mask
    following[...] = jnp.zeros_like(following)
    state_back[...] = jnp.zeros_like(state_back)
    channel_ref[...] = jnp.zeros_like(channel_ref)

    taps, bias = consts_ref[0:CONV], consts_ref[CONV : CONV + 1]
    skip = consts_ref[SKIP_ROW : SKIP_ROW + 1]
    row_at = lax.broadcasted_iota(jnp.int32, (rows, rows), 0)
    lane_at = lax.broadcasted_iota(jnp.int32, (rows, rows), 1)
    causal, causal_t = row_at >= lane_at, lane_at >= row_at

    def chunk(lap, carry):
        c = chunks - 1 - lap
        start = pl.multiple_of(c * rows, rows)
        here = pl.ds(start, rows)
        window = padded[pl.ds(start, rows + 8), :]
        pre = filtered(window, taps, bias, rows)
        gate = jax.nn.sigmoid(pre)
        values = pre * gate * mask
        columns = column_ref[here, :]
        log_full, log_lanes = head_lanes(columns, 0)
        step_lanes = head_lanes(columns, STEP_LANE)[1]
        weighted = step_lanes * values
        weighted_low = weighted.astype(bf16)
        keys, queries, queries_t = key_ref[here, :], query_ref[here, :], query_t_ref[:, here]
        grad_low = grad_ref[here, :]
        grad = grad_low.astype(f32)
        inner, inner_t = dot_lanes(queries, keys), dot_lanes(keys, queries)
        blocks = block_ref[...]
        weighted_blocks = stacked_heads(weighted_low, blocks)
        grad_blocks = stacked_heads(grad_low, blocks)
        mixing_grad = dot_lanes(grad_low, weighted_blocks)
        mixing, mixing_t, inner_sum = [], [], jnp.zeros((rows, rows), f32)
        for j in range(GROUP):
            log_row = row_ref[j : j + 1, here]
            decay = jnp.where(causal, jnp.exp(log_full[j] - log_row), 0.0)
            decay_t = jnp.where(causal_t, jnp.exp(log_row - log_full[j]), 0.0)
            mixing.append((decay * inner).astype(bf16))
            mixing_t.append((decay_t * inner_t).astype(bf16))
            inner_sum = inner_sum + decay * mixing_grad[:, j * rows : (j + 1) * rows]
        inner_grad[pl.ds(c, 1)] = inner_grad[pl.ds(c, 1)] + inner_sum[None]
        y = dot_rows(jnp.concatenate(mixing, axis=1), weighted_blocks)
        state_low = states_ref[pl.ds(c, 1)][0]
        entry = jnp.exp(log_lanes)
        y = y + entry * dot_rows(queries, state_low)
        inside = dot_rows(jnp.concatenate(mixing_t, axis=1), grad_blocks)
        back = state_back[...]
        back_low = back.astype(bf16)
        log_last = log_lanes[rows - 1 : rows, :]
        tail = jnp.exp(log_last - log_lanes)
        outside = tail * dot_rows(keys, back_low)
        entry_grad = (grad * entry).astype(bf16)
        tail_low = (weighted * tail).astype(bf16)
        query_grad_ref[here, :] = query_grad_ref[here, :] + dot_lanes(entry_grad, state_low)
        key_grad_ref[here, :] = key_grad_ref[here, :] + dot_lanes(tail_low, back_low)
        last = jnp.exp(log_last)
        rest_ref[pl.ds(c, 1)] = (
            last * jnp.sum(state_low.astype(f32) * back, axis=0, keepdims=True)
        )[None]
        state_back[...] = last * back + dot_rows(queries_t, entry_grad)
        weighted_grad = inside + outside
        first = grad * y - weighted_low.astype(f32) * inside
        first_high = first.astype(bf16)
        first_rest = (first - first_high.astype(f32)).astype(bf16)
        sums_ref[here, :] = sums_ref[here, :] + (
            dot_rows(first_high, pick_ref[0])
            + dot_rows(first_rest, pick_ref[0])
            + dot_rows((weighted * outside).astype(bf16), pick_ref[1])
            + dot_rows((values * weighted_grad).astype(bf16), pick_ref[2])
        )
        values_grad = step_lanes * weighted_grad + skip * grad
        pre_grad = values_grad * mask * (gate * (1.0 + pre * (1.0 - gate)))
        channel_ref[CONV : CONV + 1, :] += jnp.sum(pre_grad, axis=0, keepdims=True)
        channel_ref[CONV + 1 : CONV + 2, :] += jnp.sum(grad * values, axis=0, keepdims=True)
        for k in range(CONV):
            channel_ref[k : k + 1, :] += jnp.sum(
                pre_grad * window[5 + k : 5 + k + rows], axis=0, keepdims=True
            )
        ahead = jnp.concatenate([pre_grad, following[...]], axis=0)
        following[...] = pre_grad[0:8]
        x_grad = taps[CONV - 1 : CONV] * ahead[0:rows]
        for k in range(CONV - 1):
            x_grad = x_grad + taps[k : k + 1] * ahead[CONV - 1 - k : CONV - 1 - k + rows]
        x_grad_ref[here, :] = (x_grad * mask).astype(bf16)
        return carry

    lax.fori_loop(0, chunks, chunk, 0)


def scan_backward_start(key_grad_ref, query_grad_ref, sums_ref, inner_grad):
    key_grad_ref[...] = jnp.zeros_like(key_grad_ref)
    query_grad_ref[...] = jnp.zeros_like(query_grad_ref)
    inner_grad[...] = jnp.zeros_like(inner_grad)
    sums_ref[...] = jnp.zeros_like(sums_ref)


def scan_backward_finish(key_ref, query_ref, key_grad_ref, query_grad_ref, inner_grad):
    rows = SPAN

    def finish(c, carry):
        here = pl.ds(pl.multiple_of(c * rows, rows), rows)
        inner_low = inner_grad[pl.ds(c, 1)][0].astype(bf16)
        query_grad_ref[here, :] = query_grad_ref[here, :] + dot_rows(inner_low, key_ref[here, :])
        key_grad_ref[here, :] = key_grad_ref[here, :] + lax.dot_general(
            inner_low, query_ref[here, :], (((0,), (0,)), ((), ())), preferred_element_type=f32
        )
        return carry

    lax.fori_loop(0, key_ref.shape[0] // rows, finish, 0)


def scan_backward_kernel(*refs):
    key_ref, query_ref = refs[4:6]
    key_grad_ref, query_grad_ref, sums_ref = refs[12:15]
    inner_grad = refs[-1]

    @pl.when(pl.program_id(0) == 0)
    def _():
        scan_backward_start(key_grad_ref, query_grad_ref, sums_ref, inner_grad)

    scan_backward_group(*refs)

    @pl.when(pl.program_id(0) == pl.num_programs(0) - 1)
    def _():
        scan_backward_finish(key_ref, query_ref, key_grad_ref, query_grad_ref, inner_grad)


def block_mask():
    row = np.arange(GROUP * SPAN)[:, None] // SPAN
    lane = np.arange(LANES)[None, :] // HEAD_DIM
    return jnp.asarray((row == lane).astype(np.float32), bf16)


def pick_masks(groups):
    lane = np.arange(LANES)[:, None] // HEAD_DIM
    target = np.arange(PAIR)[None, :]
    masks = [
        target == (kind * groups + group) * GROUP + lane
        for group in range(groups)
        for kind in range(3)
    ]
    return jnp.asarray(np.stack(masks).astype(np.float32), bf16)


def whole_spec():
    return pl.BlockSpec(memory_space=pltpu.VMEM)


def lane_spec(rows):
    return pl.BlockSpec((rows, LANES), lambda g: (0, g))


def head_specs(length):
    return [
        lane_spec(length),
        lane_spec(8),
        pl.BlockSpec((length, PAIR), lambda g: (0, g)),
        pl.BlockSpec((8, length), lambda g: (g, 0)),
        whole_spec(),
        whole_spec(),
        whole_spec(),
        whole_spec(),
    ]


def scan_forward(x, consts, columns, rows, keys, queries, keys_t):
    length, width = x.shape
    chunks = length // SPAN
    return pl.pallas_call(
        scan_forward_kernel,
        grid=(width // LANES,),
        in_specs=head_specs(length),
        out_specs=[
            lane_spec(length),
            pl.BlockSpec((chunks, STATE, LANES), lambda g: (0, 0, g)),
        ],
        out_shape=[
            jax.ShapeDtypeStruct((length, width), f32),
            jax.ShapeDtypeStruct((chunks, STATE, width), bf16),
        ],
        scratch_shapes=[pltpu.VMEM((length + 8, LANES), f32), pltpu.VMEM((STATE, LANES), f32)],
        compiler_params=pltpu.CompilerParams(vmem_limit_bytes=VMEM_BYTES),
        cost_estimate=pl.CostEstimate(
            flops=10_000_000_000, bytes_accessed=12_000_000, transcendentals=4_000_000
        ),
        name="scan_forward",
    )(x, consts, columns, rows, keys, queries, keys_t, block_mask())


def scan_backward(
    x, consts, columns, rows, keys, queries, queries_t, grad, states
):
    length, width = x.shape
    chunks = length // SPAN
    groups = width // LANES
    same = lambda g: (0, 0)
    return pl.pallas_call(
        scan_backward_kernel,
        grid=(groups,),
        in_specs=head_specs(length)
        + [
            pl.BlockSpec((3, LANES, PAIR), lambda g: (g, 0, 0)),
            lane_spec(length),
            pl.BlockSpec((chunks, STATE, LANES), lambda g: (0, 0, g)),
        ],
        out_specs=[
            lane_spec(length),
            pl.BlockSpec((length, STATE), same),
            pl.BlockSpec((length, STATE), same),
            pl.BlockSpec((length, PAIR), same),
            pl.BlockSpec((chunks, 1, LANES), lambda g: (0, 0, g)),
            lane_spec(8),
        ],
        out_shape=[
            jax.ShapeDtypeStruct((length, width), bf16),
            jax.ShapeDtypeStruct((length, STATE), f32),
            jax.ShapeDtypeStruct((length, STATE), f32),
            jax.ShapeDtypeStruct((length, PAIR), f32),
            jax.ShapeDtypeStruct((chunks, 1, width), f32),
            jax.ShapeDtypeStruct((8, width), f32),
        ],
        scratch_shapes=[
            pltpu.VMEM((length + 8, LANES), f32),
            pltpu.VMEM((8, LANES), f32),
            pltpu.VMEM((STATE, LANES), f32),
            pltpu.VMEM((chunks, SPAN, SPAN), f32),
        ],
        compiler_params=pltpu.CompilerParams(vmem_limit_bytes=VMEM_BYTES),
        cost_estimate=pl.CostEstimate(
            flops=30_000_000_000, bytes_accessed=16_000_000, transcendentals=8_000_000
        ),
        name="scan_backward",
    )(
        x, consts, columns, rows, keys, queries, queries_t, block_mask(),
        pick_masks(groups), grad, states,
    )


def gate_kernel(
    normed_ref, weight_ref, cotangent_ref, out_ref, y_ref, gain_ref, mask_ref,
    gate_part_ref, gated_grad_ref, stats_ref,
):
    gate_part = dot_rows(normed_ref[...], weight_ref[...]) * mask_ref[...]
    gated_grad = dot_lanes(cotangent_ref[...], out_ref[...])
    gate_part_ref[...] = gate_part
    gated_grad_ref[...] = gated_grad
    gated = y_ref[...] * (gate_part * jax.nn.sigmoid(gate_part))
    squares = jnp.sum(gated * gated, axis=1, keepdims=True)
    products = jnp.sum(gated * gated_grad * gain_ref[...], axis=1, keepdims=True)
    lane = lax.broadcasted_iota(jnp.int32, stats_ref.shape, 1)
    stats_ref[...] = jnp.where(lane == 0, squares, products)


def gate_forward(normed, weight, cotangent, out_weight, y, gain, mask):
    length, width = y.shape
    rows = lambda lanes: pl.BlockSpec((ROW_TILE, lanes), lambda i: (i, 0))
    return pl.pallas_call(
        gate_kernel,
        grid=(length // ROW_TILE,),
        in_specs=[
            rows(D), whole_spec(), rows(D), whole_spec(), rows(width), whole_spec(), whole_spec(),
        ],
        out_specs=[rows(width), rows(width), rows(PAIR)],
        out_shape=[
            jax.ShapeDtypeStruct((length, width), f32),
            jax.ShapeDtypeStruct((length, width), f32),
            jax.ShapeDtypeStruct((length, PAIR), f32),
        ],
        compiler_params=pltpu.CompilerParams(vmem_limit_bytes=VMEM_BYTES),
        cost_estimate=pl.CostEstimate(
            flops=9_000_000_000, bytes_accessed=28_000_000, transcendentals=1_000_000
        ),
        name="gate_forward",
    )(normed, weight, cotangent, out_weight, y, gain, mask)


def norm_back_kernel(
    y_ref, gate_part_ref, gated_grad_ref, scale_ref, gain_ref, mask_ref,
    gated_ref, y_grad_ref, gate_grad_ref, gain_grad_ref,
):
    @pl.when(pl.program_id(0) == 0)
    def _():
        gain_grad_ref[...] = jnp.zeros_like(gain_grad_ref)

    y, gate_part, gated_grad = y_ref[...], gate_part_ref[...], gated_grad_ref[...]
    inverse, pull = scale_ref[:, 0:1], scale_ref[:, 1:2]
    gate = jax.nn.sigmoid(gate_part)
    silu = gate_part * gate
    gated = y * silu
    scaled = gated * inverse
    gain = gain_ref[...]
    gated_ref[...] = (scaled * gain).astype(bf16)
    gain_grad_ref[0:1, :] += jnp.sum(gated_grad * scaled, axis=0, keepdims=True)
    back = inverse * (gated_grad * gain) - gated * pull
    y_grad_ref[...] = (back * silu).astype(bf16)
    gate_grad_ref[...] = (
        back * y * (gate * (1.0 + gate_part * (1.0 - gate))) * mask_ref[...]
    ).astype(bf16)


def norm_back(y, gate_part, gated_grad, scales, gain, mask):
    length, width = y.shape
    rows = lambda lanes: pl.BlockSpec((ROW_TILE, lanes), lambda i: (i, 0))
    return pl.pallas_call(
        norm_back_kernel,
        grid=(length // ROW_TILE,),
        in_specs=[rows(width), rows(width), rows(width), rows(2), whole_spec(), whole_spec()],
        out_specs=[
            rows(width), rows(width), rows(width), pl.BlockSpec((8, width), lambda i: (0, 0)),
        ],
        out_shape=[
            jax.ShapeDtypeStruct((length, width), bf16),
            jax.ShapeDtypeStruct((length, width), bf16),
            jax.ShapeDtypeStruct((length, width), bf16),
            jax.ShapeDtypeStruct((8, width), f32),
        ],
        compiler_params=pltpu.CompilerParams(vmem_limit_bytes=VMEM_BYTES),
        cost_estimate=pl.CostEstimate(
            flops=30_000_000, bytes_accessed=18_000_000, transcendentals=1_000_000
        ),
        name="norm_back",
    )(y, gate_part, gated_grad, scales, gain, mask)


MESH = pl.DeviceIdType.MESH


class Ring:
    def __init__(self):
        self.count = lax.axis_size("dp")
        self.far = self.count // 2
        me = lax.axis_index("dp")
        odd = lax.rem(me, 2)
        self.me = me
        self.place = (1 - odd) * lax.div(me, 2) + odd * lax.div(2 * self.count - 1 - me, 2)

    def member(self, distance):
        n = self.count
        place = lax.rem(self.place + distance + n, n)
        back = lax.div(place, n // 2)
        return (1 - back) * 2 * place + back * (2 * n - 1 - 2 * place)

    def target(self, way):
        return {"dp": self.member(1 if way == 0 else -1)}


def partner(flip):
    f = lax.axis_index("fsdp")
    return (f, f + 1 - 2 * lax.rem(f, 2), lax.rem(f + 2, 4), 3 - f)[flip]


def greet(targets):
    barrier = pltpu.get_barrier_semaphore()
    for target in targets:
        pl.semaphore_signal(barrier, inc=1, device_id=target, device_id_type=MESH)
    pl.semaphore_wait(barrier, len(targets))


def row_slice(ref, start, size):
    return ref.at[pl.ds(pl.multiple_of(start, 16), size)]


class RingGather:
    def __init__(self, ring, wholes, send, recv):
        self.ring, self.wholes, self.send, self.recv = ring, wholes, send, recv

    @staticmethod
    def semaphores(parts, count):
        return pltpu.SemaphoreType.DMA((parts * 4 * (count // 2),))

    def copy(self, part, way, half, hop):
        whole = self.wholes[part]
        rows = whole.shape[0] // self.ring.count
        size = rows // 2
        owner = self.ring.member(-hop if way == 0 else hop)
        place = row_slice(whole, owner * rows + half * size, size)
        at = ((part * 2 + way) * 2 + half) * self.ring.far + hop
        return pltpu.make_async_remote_copy(
            place, place, self.send.at[at], self.recv.at[at],
            device_id=self.ring.target(way), device_id_type=MESH,
        )

    def pieces(self, hop):
        return [
            (way, half)
            for half in (0, 1)
            for way in (0, 1)
            if hop < self.ring.far - 1 or half == way
        ]

    def start(self, part, hop):
        for way, half in self.pieces(hop):
            if hop:
                self.copy(part, way, half, hop - 1).wait_recv()
            self.copy(part, way, half, hop).start()

    def finish(self, part):
        last = self.ring.far - 1
        for way, half in self.pieces(last):
            self.copy(part, way, half, last).wait_recv()
            if last:
                self.copy(part, way, 1 - half, last - 1).wait_recv()
        for hop in range(last + 1):
            for way, half in self.pieces(hop):
                self.copy(part, way, half, hop).wait_send()


class RingScatter:
    def __init__(self, ring, held, arrived, send, recv):
        self.ring, self.held, self.arrived = ring, held, arrived
        self.send, self.recv = send, recv

    @staticmethod
    def scratch(count, rows, columns):
        return [
            pltpu.VMEM((2, 2, rows, columns), bf16),
            pltpu.VMEM((2, count // 2 * rows - rows // 2, columns), bf16),
        ]

    def landing(self, way, hop):
        rows = self.held.shape[2]
        if hop == 0:
            return self.arrived.at[way, pl.ds((self.ring.far - 1) * rows, rows // 2)]
        return self.arrived.at[way, pl.ds((hop - 1) * rows, rows)]

    def copy(self, way, hop):
        rows = self.held.shape[2]
        size = rows // 2 if hop == 0 else rows
        at = way * self.ring.far + hop
        return pltpu.make_async_remote_copy(
            self.held.at[way, hop % 2, pl.ds(0, size)], self.landing(way, hop),
            self.send.at[at], self.recv.at[at],
            device_id=self.ring.target(way), device_id_type=MESH,
        )

    def owner(self, way, hop):
        distance = self.ring.far - hop
        return self.ring.member(distance if way == 0 else -distance)

    def start(self, hop, term):
        rows = self.held.shape[2]
        half = rows // 2
        if hop == 0:
            value = term(self.owner(0, 0), 0).astype(bf16)
            self.held[0, 0, 0:half] = value[:half]
            self.copy(0, 0).start()
            self.held[1, 0, 0:half] = value[half:]
            self.copy(1, 0).start()
            return
        for way in (0, 1):
            value = term(self.owner(way, hop), way)
            self.copy(way, hop - 1).wait_recv()
            slot = hop % 2
            if hop >= 2:
                self.copy(way, hop - 2).wait_send()
            if hop == 1:
                low = slice(way * half, (way + 1) * half)
                rest = slice((1 - way) * half, (2 - way) * half)
                self.held[way, slot, low] = (
                    value[low] + self.landing(way, 0)[...].astype(f32)
                ).astype(bf16)
                self.held[way, slot, rest] = value[rest].astype(bf16)
            else:
                self.held[way, slot] = (
                    value + self.landing(way, hop - 1)[...].astype(f32)
                ).astype(bf16)
            self.copy(way, hop).start()

    def finish(self, term):
        last = self.ring.far - 1
        value = term(self.ring.me, 0)
        for way in (0, 1):
            self.copy(way, last).wait_recv()
            value = value + self.landing(way, last)[...].astype(f32)
        for hop in range(last - 1, last + 1):
            for way in (0, 1):
                self.copy(way, hop).wait_send()
        return value


def any_specs(count):
    return [pl.BlockSpec(memory_space=pl.ANY)] * count


def tokens_exchange(own, whole, send, recv, base):
    f = lax.axis_index("fsdp")
    rows = whole.shape[0] // 4

    def one(at, source, owner, k):
        return pltpu.make_async_remote_copy(
            source, row_slice(whole, owner * rows, rows), send.at[base + at], recv.at[base + at],
            device_id={"fsdp": partner(k)}, device_id_type=MESH,
        )

    far = partner(2)
    return (
        one(0, own, f, 2), one(1, own, f, 1), one(2, row_slice(whole, far * rows, rows), far, 1),
    )


def forward_kernel(
    tokens_ref, cotangent_hbm, in_ref, out_ref, turn_ref, vectors_ref, active_ref, block_ref,
    small_all, x_all, gate_all, out_all, cotangent_all, normed_t_all, x_part_all, states_all,
    gated_all, gated_t_all, y_grad_all, gate_grad_all,
    consts_ref, head_ref, shared_taps_ref, columns_ref, rows_ref, column_ref, keys_ref, queries_ref, queries_t_ref,
    shared_part_ref, shared_pre_ref, gain_grad_ref,
    small_cut, x_cut, gate_cut, out_low, normed, cotangent, small_weight, keys_t, shared_all,
    x_part, states, y, gate_part, gated_grad, weight, out_tile, turned, squares, products, stats, stats_in,
    back_tiles, back_tiles_t, padded, state, shared_wide,
    local_sem, swap_send, swap_recv, token_send, token_recv, ring_send, ring_recv,
    shared_send, shared_recv, stats_send, stats_recv, load_sem, store_sem,
):
    ring = Ring()
    d, f = ring.me, lax.axis_index("fsdp")
    tokens, length = tokens_ref.shape[0], normed.shape[0]
    sub, rows_out = in_ref.shape[0], out_ref.shape[0]
    width = x_cut.shape[2]
    groups, chunks = width // LANES, length // SPAN
    heads, shared = HEADS // 4, shared_taps_ref.shape[0]
    precise = partial(jnp.dot, precision=highest, preferred_element_type=f32)
    greet([{"fsdp": partner(k)} for k in (1, 2, 3)] + [ring.target(0), ring.target(1)])
    wholes = [small_all, x_all, gate_all, out_all]
    small_part, x_of, gate_of, out_of = range(4)
    rings = RingGather(ring, wholes, ring_send, ring_recv)
    cuts = [small_cut, x_cut, gate_cut]

    def own_copy(part):
        if part == out_of:
            source, target = out_low, row_slice(out_all, d * rows_out, rows_out)
        else:
            source = cuts[part].at[f]
            target = row_slice(wholes[part], (4 * d + f) * sub, sub)
        return pltpu.make_async_copy(source, target, local_sem.at[part])

    def swap(part, k):
        return pltpu.make_async_remote_copy(
            cuts[part].at[partner(k)], row_slice(wholes[part], (4 * d + f) * sub, sub),
            swap_send.at[3 * part + k - 1], swap_recv.at[3 * part + k - 1],
            device_id={"fsdp": partner(k)}, device_id_type=MESH,
        )

    def start_swaps(part):
        for k in (2, 3, 1):
            swap(part, k).start()
        own_copy(part).start()

    def start_ring(part):
        own_copy(part).wait()
        if part != out_of:
            for k in (1, 2, 3):
                swap(part, k).wait_recv()
        rings.start(part, 0)

    def cut_channels(target, low):
        for pair in range(INNER // PAIR):
            member, at = pair % 4, pair // 4
            target[member, :, at * PAIR : (at + 1) * PAIR] = in_ref[
                :, low + pair * PAIR : low + (pair + 1) * PAIR
            ].astype(bf16)

    out_low[...] = out_ref[...].astype(bf16)
    own_copy(out_of).start()
    pieces = dot_lanes(in_ref[:, 2 * INNER :].astype(bf16), turn_ref[...]).astype(bf16)
    for member in range(4):
        small_cut[member] = pieces[:, member * PAIR : (member + 1) * PAIR]
    start_swaps(small_part)
    cut_channels(x_cut, INNER)
    start_swaps(x_of)
    start_ring(out_of)
    inputs = tokens_ref[...].astype(f32)
    inverse = lax.rsqrt(jnp.sum(inputs * inputs, axis=1, keepdims=True) / D + norm_eps)
    own_rows = pl.ds(pl.multiple_of(f * tokens, tokens), tokens)
    normed[own_rows, :] = (inputs * inverse * norm_gain_row(vectors_ref)).astype(bf16)
    normed_copies = tokens_exchange(normed.at[own_rows], normed, token_send, token_recv, 0)
    cotangent_copies = tokens_exchange(
        cotangent_hbm, cotangent, token_send, token_recv, 3
    )
    cotangent_own = pltpu.make_async_copy(cotangent_hbm, cotangent.at[own_rows], local_sem.at[4])
    cotangent_own.start()
    for copy in normed_copies[:2]:
        copy.start()
    start_ring(small_part)
    start_ring(x_of)
    cut_channels(gate_cut, 0)
    start_swaps(gate_of)

    def vector_row(row):
        return vectors_ref[pl.ds(row, 1), :]

    def own_channels(first_row):
        return jnp.concatenate(
            [vector_row(first_row + 4 * pair + f) for pair in range(width // PAIR)], axis=1
        )

    active = active_ref[0:1, 0:1]
    for k in range(CONV + 1):
        consts_ref[k : k + 1, :] = own_channels(TAPS_ROW + k * (XBC // PAIR))
    channel_head = lax.broadcasted_iota(jnp.int32, (1, width), 1) // HEAD_DIM
    consts_ref[MASK_ROW : MASK_ROW + 1, :] = (channel_head.astype(f32) < active / 4).astype(f32)
    consts_ref[GAIN_ROW : GAIN_ROW + 1, :] = own_channels(D // PAIR)
    head_at = lax.broadcasted_iota(jnp.int32, (PAIR, PAIR), 0)
    local_at = lax.broadcasted_iota(jnp.int32, (PAIR, PAIR), 1)
    own_head = local_at // 2 * 8 + 2 * f + local_at % 2
    chosen = (head_at == own_head) & (local_at < heads)
    chosen_far = (head_at == own_head + HEADS) & (local_at < heads)
    last = vector_row(LAST_ROW)
    step_bias_row = precise(last, chosen.astype(f32))
    is_head = lax.broadcasted_iota(jnp.int32, (1, PAIR), 1) < heads
    decay_row = jnp.where(is_head, -jnp.exp(precise(last, chosen_far.astype(f32))), 0.0)
    head_mask_row = (
        lax.broadcasted_iota(jnp.int32, (1, PAIR), 1).astype(f32) < active / 4
    ).astype(f32)
    skip_row = precise(vector_row(LAST_ROW + 1), chosen.astype(f32))
    spread_head = (
        lax.broadcasted_iota(jnp.int32, (PAIR, width), 0)
        == lax.broadcasted_iota(jnp.int32, (PAIR, width), 1) // HEAD_DIM
    ).astype(f32)
    consts_ref[SKIP_ROW : SKIP_ROW + 1, :] = precise(skip_row, spread_head)
    head_ref[...] = jnp.concatenate(
        [decay_row, head_mask_row, step_bias_row, jnp.zeros((5, PAIR), f32)], axis=0
    )
    shared_rows = [
        vector_row(TAPS_ROW + k * (XBC // PAIR) + INNER // PAIR + f // 2) for k in range(CONV + 1)
    ]
    shared_wide[...] = jnp.concatenate(
        shared_rows + [jnp.zeros((PAIR - CONV - 1, PAIR), f32)], axis=0
    ).T
    shared_taps_ref[...] = shared_wide[pl.ds(pl.multiple_of(f % 2 * shared, shared), shared), :]
    rings.start(small_part, 1)
    rings.start(small_part, 2)
    rings.start(x_of, 1)
    rings.start(out_of, 1)
    for hop in range(3, ring.far):
        rings.start(small_part, hop)
    normed_copies[0].wait_recv()
    normed_copies[2].start()
    for copy in cotangent_copies[:2]:
        copy.start()
    rings.finish(small_part)
    load_small = pltpu.make_async_copy(small_all, small_weight, local_sem.at[5])
    load_small.start()
    for copy in normed_copies[1:]:
        copy.wait_recv()
    load_small.wait()

    small = dot_rows(normed[...], small_weight[...]).T
    part = small[0:shared]
    pre = shared_taps_ref[:, CONV : CONV + 1] + jnp.zeros_like(part)
    for k in range(CONV):
        pre = pre + shared_taps_ref[:, k : k + 1] * shifted(part, CONV - 1 - k)
    shared_part_ref[...] = part
    shared_pre_ref[...] = pre
    shared_all[f] = (pre * jax.nn.sigmoid(pre)).astype(bf16)

    def shared_copy(k):
        return pltpu.make_async_remote_copy(
            shared_all.at[f], shared_all.at[f], shared_send.at[k - 1], shared_recv.at[k - 1],
            device_id={"fsdp": partner(k)}, device_id_type=MESH,
        )

    for k in (2, 3, 1):
        shared_copy(k).start()
    rings.start(x_of, 2)
    rings.start(out_of, 2)
    head_columns = jnp.concatenate(
        [head_ref[...], jnp.zeros((PAIR - 8, PAIR), f32)], axis=0
    ).T[0:heads]
    decay, head_mask, step_bias = (head_columns[:, i : i + 1] for i in range(3))
    logits = small[shared : shared + heads] * head_mask + step_bias
    steps = jnp.maximum(logits, 0.0) + jnp.log1p(jnp.exp(-jnp.abs(logits)))
    at_row = lax.broadcasted_iota(jnp.int32, (SPAN, SPAN), 0)
    at_lane = lax.broadcasted_iota(jnp.int32, (SPAN, SPAN), 1)
    upto = (at_row <= at_lane).astype(f32)
    rates = steps * decay
    log_sums = jnp.concatenate(
        [
            jnp.dot(
                rates[:, c * SPAN : (c + 1) * SPAN], upto, precision=highest,
                preferred_element_type=f32,
            )
            for c in range(chunks)
        ],
        axis=1,
    )
    column = jnp.concatenate(
        [log_sums, steps, logits, jnp.zeros((PAIR - 3 * heads, length), f32)], axis=0
    ).T
    column_ref[...] = column
    for group in range(groups):
        rolled = column if group == 0 else pltpu.roll(column, PAIR - group * GROUP, 1)
        columns_ref[:, group * PAIR : (group + 1) * PAIR] = rolled
        rows_ref[group * 8 : group * 8 + 8, :] = jnp.zeros((8, length), f32)
        rows_ref[group * 8 : group * 8 + GROUP, :] = log_sums[group * GROUP : (group + 1) * GROUP]
    for k in (1, 2, 3):
        shared_copy(k).wait_recv()
    keys_t[0:shared, :] = shared_all[0]
    keys_t[shared:, :] = shared_all[1]
    queries_t_ref[0:shared, :] = shared_all[2]
    queries_t_ref[shared:, :] = shared_all[3]
    keys_ref[...] = keys_t[...].T
    queries_ref[...] = queries_t_ref[...].T
    for hop in range(3, ring.far):
        rings.start(x_of, hop)
        rings.start(out_of, hop)
    cotangent_copies[0].wait_recv()
    cotangent_copies[2].start()

    def store(source, target, slot):
        return pltpu.make_async_copy(source, target, store_sem.at[slot])

    quarter = D // 4

    def turned_store(i):
        return store(turned.at[i % 2], row_slice(normed_t_all, i * quarter, quarter), i)

    for i in range(4):
        if i >= 2:
            turned_store(i - 2).wait()
        turned[i % 2] = normed[:, i * quarter : (i + 1) * quarter].T
        turned_store(i).start()
    rings.finish(x_of)
    start_ring(gate_of)

    def lanes(group):
        return pl.ds(group * LANES, LANES)

    def load_columns(source, group):
        return pltpu.make_async_copy(
            source.at[:, lanes(group)], weight.at[group % 2], load_sem.at[group % 2]
        )

    def x_store(group):
        return store(x_part.at[group % 2], x_part_all.at[:, lanes(group)], 4 + group)

    def states_store(group):
        return store(states.at[group % 2], states_all.at[:, :, lanes(group)], 8 + group)

    load_columns(x_all, 0).start()
    for group in range(groups):
        if group + 1 < groups:
            load_columns(x_all, group + 1).start()
        load_columns(x_all, group).wait()
        if group >= 2:
            x_store(group - 2).wait()
            states_store(group - 2).wait()
        slot = group % 2
        x_part[slot] = dot_rows(normed[...], weight[slot])
        x_store(group).start()
        scan_forward_kernel(
            x_part.at[slot], consts_ref.at[:, lanes(group)],
            columns_ref.at[:, pl.ds(group * PAIR, PAIR)], rows_ref.at[pl.ds(group * 8, 8)],
            keys_ref, queries_ref, keys_t, block_ref, y.at[:, lanes(group)], states.at[slot],
            padded, state,
        )
        states_store(group).start()
        if group % 2 == 1 and group // 2 + 1 < ring.far - 1:
            rings.start(gate_of, group // 2 + 1)

    for copy in cotangent_copies[1:]:
        copy.wait_recv()
    cotangent_own.wait()
    cotangent_store = store(cotangent, cotangent_all, 12)
    cotangent_store.start()
    rings.finish(out_of)

    def load_rows(group):
        return pltpu.make_async_copy(
            out_all.at[lanes(group)], out_tile.at[group % 2], load_sem.at[2 + group % 2]
        )

    load_rows(0).start()
    for group in range(groups):
        if group + 1 < groups:
            load_rows(group + 1).start()
        load_rows(group).wait()
        gated_grad[:, lanes(group)] = dot_lanes(cotangent[...], out_tile[group % 2])
    rings.start(gate_of, ring.far - 1)
    rings.finish(gate_of)

    def const_row(row, here):
        return consts_ref[row : row + 1, here]

    load_columns(gate_all, 0).start()
    for group in range(groups):
        if group + 1 < groups:
            load_columns(gate_all, group + 1).start()
        load_columns(gate_all, group).wait()
        here = lanes(group)
        value = dot_rows(normed[...], weight[group % 2]) * const_row(MASK_ROW, here)
        gate_part[:, here] = value
        gated = y[:, here] * (value * jax.nn.sigmoid(value))
        product = gated * (gated_grad[:, here] * const_row(GAIN_ROW, here))
        gated = gated * gated
        gated = gated[:, :PAIR] + gated[:, PAIR:]
        product = product[:, :PAIR] + product[:, PAIR:]
        squares[...] = gated if group == 0 else squares[...] + gated
        products[...] = product if group == 0 else products[...] + product
    lane = lax.broadcasted_iota(jnp.int32, (length, PAIR), 1)
    both = jnp.where(
        lane == 0,
        jnp.sum(squares[...], axis=1, keepdims=True),
        jnp.where(lane == 1, jnp.sum(products[...], axis=1, keepdims=True), 0.0),
    )
    stats[...] = both.T[0:8]

    def stats_copy(k):
        return pltpu.make_async_remote_copy(
            stats, stats_in.at[k - 1], stats_send.at[k - 1], stats_recv.at[k - 1],
            device_id={"fsdp": partner(k)}, device_id_type=MESH,
        )

    for k in (2, 3, 1):
        stats_copy(k).start()
    for k in (1, 2, 3):
        stats_copy(k).wait_recv()
    total = (stats[...] + stats_in[0]) + (stats_in[1] + stats_in[2])
    channel_count = active * HEAD_DIM
    inverse_out = lax.rsqrt(total[0:1] / channel_count + norm_eps)
    pulls = inverse_out * inverse_out * inverse_out / channel_count * total[1:2]
    scales = jnp.concatenate(
        [inverse_out, pulls, jnp.zeros((PAIR - 2, length), f32)], axis=0
    ).T
    inverse_out, pulls = scales[:, 0:1], scales[:, 1:2]

    def back_stores(group):
        slot, at, here = group % 2, 13 + 4 * group, lanes(group)
        return [
            store(back_tiles.at[slot, 0], gated_all.at[:, here], at),
            store(back_tiles.at[slot, 1], y_grad_all.at[:, here], at + 1),
            store(back_tiles.at[slot, 2], gate_grad_all.at[:, here], at + 2),
            store(back_tiles_t.at[slot], gated_t_all.at[here], at + 3),
        ]

    gain_grad_ref[...] = jnp.zeros_like(gain_grad_ref)
    for group in range(groups):
        here, slot = lanes(group), group % 2
        if group >= 2:
            for copy in back_stores(group - 2):
                copy.wait()
        value, grad, gain = gate_part[:, here], gated_grad[:, here], const_row(GAIN_ROW, here)
        gate = jax.nn.sigmoid(value)
        silu = value * gate
        y_here = y[:, here]
        gated = y_here * silu
        scaled = gated * inverse_out
        gated_low = (scaled * gain).astype(bf16)
        back_tiles[slot, 0] = gated_low
        back_tiles_t[slot] = gated_low.T
        gain_grad_ref[0:1, here] = jnp.sum(grad * scaled, axis=0, keepdims=True)
        back = inverse_out * (grad * gain) - gated * pulls
        back_tiles[slot, 1] = (back * silu).astype(bf16)
        back_tiles[slot, 2] = (
            back * y_here * (gate * (1.0 + value * (1.0 - gate))) * const_row(MASK_ROW, here)
        ).astype(bf16)
        for copy in back_stores(group):
            copy.start()

    for i in (2, 3):
        turned_store(i).wait()
    for group in range(groups - 2, groups):
        x_store(group).wait()
        states_store(group).wait()
        for copy in back_stores(group):
            copy.wait()
    cotangent_store.wait()
    for copy in normed_copies + cotangent_copies:
        copy.wait_send()
    for k in (1, 2, 3):
        shared_copy(k).wait_send()
        stats_copy(k).wait_send()
        for i in (small_part, x_of, gate_of):
            swap(i, k).wait_send()


def last_columns(members):
    shared = 2 * STATE // members
    source = np.arange(2 * STATE + HEADS)
    head = source - 2 * STATE
    target = np.where(
        source < 2 * STATE,
        source // shared * PAIR + source % shared,
        head // 2 % members * PAIR + shared + head // (2 * members) * 2 + head % 2,
    )
    turn = np.arange(members * PAIR)[:, None] == target[None, :]
    return jnp.asarray(turn.astype(np.float32), bf16)


def norm_gain_row(vectors_ref):
    return jnp.concatenate([vectors_ref[i : i + 1, :] for i in range(D // PAIR)], axis=1)


def vector_tiles(vectors):
    rows = -(-vectors.shape[0] // PAIR)
    return jnp.pad(vectors, (0, rows * PAIR - vectors.shape[0])).reshape(rows, PAIR)


def forward(
    tokens, cotangent, in_weight, out_weight, vectors, active,
):
    count, members = lax.axis_size("dp"), lax.axis_size("fsdp")
    own, sub, rows_out = tokens.shape[0], in_weight.shape[0], out_weight.shape[0]
    length, inner, shared = own * members, INNER // members, 2 * STATE // members
    chunks, groups = length // SPAN, inner // LANES
    assert groups == 4 and count == 8 and members == 4
    turn = last_columns(members)
    sd, dma = jax.ShapeDtypeStruct, pltpu.SemaphoreType.DMA
    vmem = pltpu.VMEM
    return pl.pallas_call(
        forward_kernel,
        in_specs=[whole_spec()] + any_specs(1) + [whole_spec()] * 6,
        out_specs=any_specs(12) + [whole_spec()] * 12,
        out_shape=[
            sd((D, PAIR), bf16),
            sd((D, inner), bf16),
            sd((D, inner), bf16),
            sd((inner, D), bf16),
            sd((length, D), bf16),
            sd((D, length), bf16),
            sd((length, inner), f32),
            sd((chunks, STATE, inner), bf16),
            sd((length, inner), bf16),
            sd((inner, length), bf16),
            sd((length, inner), bf16),
            sd((length, inner), bf16),
            sd((8, inner), f32),
            sd((8, PAIR), f32),
            sd((shared, PAIR), f32),
            sd((length, groups * PAIR), f32),
            sd((groups * 8, length), f32),
            sd((length, PAIR), f32),
            sd((length, STATE), bf16),
            sd((length, STATE), bf16),
            sd((STATE, length), bf16),
            sd((shared, length), f32),
            sd((shared, length), f32),
            sd((8, inner), f32),
        ],
        scratch_shapes=[
            vmem((members, sub, PAIR), bf16),
            vmem((members, sub, inner), bf16),
            vmem((members, sub, inner), bf16),
            vmem((rows_out, D), bf16),
            vmem((length, D), bf16),
            vmem((length, D), bf16),
            vmem((D, PAIR), bf16),
            vmem((STATE, length), bf16),
            vmem((members, shared, length), bf16),
            vmem((2, length, LANES), f32),
            vmem((2, chunks, STATE, LANES), bf16),
            vmem((length, inner), f32),
            vmem((length, inner), f32),
            vmem((length, inner), f32),
            vmem((2, D, LANES), bf16),
            vmem((2, LANES, D), bf16),
            vmem((2, D // 4, length), bf16),
            vmem((length, PAIR), f32),
            vmem((length, PAIR), f32),
            vmem((8, length), f32),
            vmem((3, 8, length), f32),
            vmem((2, 3, length, LANES), bf16),
            vmem((2, LANES, length), bf16),
            vmem((length + 8, LANES), f32),
            vmem((STATE, LANES), f32),
            vmem((PAIR, PAIR), f32),
            dma((6,)),
            dma((9,)),
            dma((9,)),
            dma((6,)),
            dma((6,)),
            RingGather.semaphores(4, count),
            RingGather.semaphores(4, count),
            dma((3,)),
            dma((3,)),
            dma((3,)),
            dma((3,)),
            dma((4,)),
            dma((13 + 4 * groups,)),
        ],
        compiler_params=pltpu.CompilerParams(
            collective_id=0, has_side_effects=True, vmem_limit_bytes=VMEM_BYTES
        ),
        name="forward",
    )(
        tokens, cotangent, in_weight, out_weight, turn, vectors,
        jnp.broadcast_to(active.astype(f32), (8, PAIR)), block_mask(),
    )


def total_squares(value):
    return jnp.sum(jnp.sum(value * value, axis=0, keepdims=True), axis=1, keepdims=True)


def flipped(member, flip):
    return member + flip - 2 * flip * lax.rem(lax.div(member, flip), 2)


def shifted(value, by):
    length = value.shape[1]
    lane = lax.broadcasted_iota(jnp.int32, value.shape, 1)
    if by == 0:
        return value
    if by > 0:
        return jnp.where(lane >= by, pltpu.roll(value, by, 1), 0.0)
    return jnp.where(lane < length + by, pltpu.roll(value, length + by, 1), 0.0)


def backward_kernel(
    rows_ref, key_ref, query_ref, query_t_ref, block_ref, pick_ref, consts_ref, column_ref, heads_ref,
    head_pick_ref, shared_part_ref, shared_pre_ref, taps_ref, vectors_own_ref, gate_gain_ref,
    weight_small_ref,
    tokens_hbm, x_hbm, y_grad_hbm, states_hbm, columns_hbm, gated_hbm, gated_t_hbm, gate_grad_hbm, normed_t_hbm,
    cotangents_hbm, cotangent_hbm, weight_out_hbm, weight_gate_hbm, weight_x_hbm,
    layer_out_hbm, token_grad_hbm, gate_back, x_back, small_back,
    out_raw_ref, vectors_ref, total_ref,
    x_part, y_grad, states, columns, padded, following, state_back, inner_grad,
    x_grad, key_grad, query_grad, sums_ref, rest_ref, channel_ref,
    normed_t, gate_grad, gated_t, cotangent, wide,
    kept, near_out, near_in,
    shared_out, shared_in, raw, small_t, small_n,
    vector_sum, vector_in, gate_out, x_out, small_out, scalar_out, scalar_in,
    first_held, first_arrived, gate_held, gate_arrived, small_held, small_arrived,
    load_sem, scan_sem, chunk_sem, store_sem, local_sem,
    near_send, near_recv, swap_send, swap_recv, vector_send, vector_recv, return_send, return_recv,
    scalar_send, scalar_recv, ring_send, ring_recv, ring_free, near_free,
):
    ring = Ring()
    d, f, count, far = ring.me, lax.axis_index("fsdp"), ring.count, ring.far
    length, width = x_grad.shape
    groups, chunks = width // LANES, length // SPAN
    rows, rows_out, tokens = D // count, width // count, tokens_hbm.shape[0]
    sub, shared, heads = gate_back.shape[1], shared_part_ref.shape[0], HEADS // 4
    precise = partial(jnp.dot, precision=highest, preferred_element_type=f32)
    out_ring, gate_ring, x_ring, small_ring = (
        RingScatter(ring, held, arrived, ring_send.at[i], ring_recv.at[i])
        for i, (held, arrived) in enumerate(
            [
                (first_held, first_arrived),
                (gate_held, gate_arrived),
                (first_held, first_arrived),
                (small_held, small_arrived),
            ]
        )
    )

    def load(source, target, at):
        return pltpu.make_async_copy(source, target, load_sem.at[at])

    def lanes(group):
        return pl.ds(group * LANES, LANES)

    def scan_loads(group):
        slot = group % 2
        return [
            pltpu.make_async_copy(source, target, scan_sem.at[slot, i])
            for i, (source, target) in enumerate(
                [
                    (y_grad_hbm.at[:, lanes(group)], y_grad.at[slot]),
                    (states_hbm.at[:, :, lanes(group)], states.at[slot]),
                    (columns_hbm.at[:, pl.ds(group * PAIR, PAIR)], columns.at[slot]),
                ]
            )
        ]

    def x_load(group):
        return pltpu.make_async_copy(x_hbm.at[:, lanes(group)], x_part, scan_sem.at[2, 0])

    def chunk_load(owner, slot):
        return pltpu.make_async_copy(
            row_slice(gated_t_hbm, owner * rows_out, rows_out), gated_t.at[slot],
            chunk_sem.at[slot],
        )

    def hop_loads(hop):
        if hop == far:
            return [chunk_load(d, 2 * (hop % 2))]
        ways = (0,) if hop == 0 else (0, 1)
        return [chunk_load(out_ring.owner(way, hop), 2 * (hop % 2) + way) for way in ways]

    gated_blocks = [x_out, gate_out]

    def gated_load(i, flip):
        return load(
            row_slice(gated_hbm, partner(flip) * tokens, tokens), gated_blocks[i], 4 + i
        )

    cotangent_load = load(cotangents_hbm, cotangent, 0)
    normed_load = load(normed_t_hbm, normed_t, 1)
    gate_grad_load = load(gate_grad_hbm, gate_grad, 2)
    out_load = load(weight_out_hbm, wide, 3)
    for copy in hop_loads(0) + [cotangent_load, normed_load, gate_grad_load, out_load]:
        copy.start()
    gated_load(0, 3).start()
    gated_load(1, 1).start()
    x_load(0).start()
    for copy in scan_loads(0):
        copy.start()
    greet(
        [{"fsdp": partner(k)} for k in (1, 2, 3)]
        + [{"dp": lax.rem(d + k, count)} for k in range(1, count)]
    )

    def rows_of(owner):
        return pl.ds(pl.multiple_of(owner * rows, rows), rows)

    def out_term(hop):
        def term(owner, way):
            value = dot_rows(gated_t[2 * (hop % 2) + way], cotangent[...])
            return jnp.concatenate([value[:, :width], value[:, width:]], axis=0)

        return term

    def out_hop(hop):
        for copy in hop_loads(hop):
            copy.wait()
        out_ring.start(hop, out_term(hop))
        for copy in hop_loads(hop + 1):
            copy.start()

    def gate_term(owner, way):
        return dot_rows(normed_t[rows_of(owner), :], gate_grad[...])

    def x_term(owner, way):
        return dot_rows(normed_t[rows_of(owner), :], x_grad[...])

    def small_term(owner, way):
        return dot_lanes(normed_t[rows_of(owner), :], small_t[...])

    def to_partner(k, source, target, send, recv, at):
        return pltpu.make_async_remote_copy(
            source, target, send.at[at], recv.at[at],
            device_id={"fsdp": partner(k)}, device_id_type=MESH,
        )

    def near_copy(use, i):
        return to_partner(
            2 if i == 2 else 1, near_out.at[i], near_in.at[i], near_send, near_recv, 3 * use + i
        )

    def scan(group):
        slot = group % 2
        x_load(group).wait()
        for copy in scan_loads(group):
            copy.wait()
        if group + 1 < groups:
            for copy in scan_loads(group + 1):
                copy.start()
        here = lanes(group)
        scan_backward_group(
            x_part, consts_ref.at[:, here], columns.at[slot], rows_ref.at[pl.ds(group * 8, 8)],
            key_ref, query_ref, query_t_ref, block_ref, pick_ref.at[pl.ds(3 * group, 3)],
            y_grad.at[slot], states.at[slot],
            x_grad.at[:, here], key_grad, query_grad, sums_ref, rest_ref.at[:, :, here],
            channel_ref.at[:, here], padded, following, state_back, inner_grad,
        )
        if group + 1 < groups:
            x_load(group + 1).start()

    scan_backward_start(key_grad, query_grad, sums_ref, inner_grad)
    cotangent_load.wait()
    out_hop(0)
    normed_load.wait()
    gate_grad_load.wait()
    gate_ring.start(0, gate_term)

    def added_block(i):
        return dot_rows(gated_blocks[i][...], wide[...])

    out_load.wait()
    for i, flip in ((0, 3), (1, 1)):
        gated_load(i, flip).wait()
        near_out[1 - i] = added_block(i).astype(bf16)
        near_copy(0, 1 - i).start()
        gated_load(i, (2, 0)[i]).start()
    scan(0)
    out_hop(1)
    gated_load(0, 2).wait()
    value = added_block(0)
    near_copy(0, 1).wait_recv()
    near_out[2] = (value + near_in[1].astype(f32)).astype(bf16)
    near_copy(0, 2).start()
    gated_load(1, 0).wait()
    kept[...] = added_block(1)
    half = D // 4

    def weight_tiles(source, target, at):
        return [
            load(
                source.at[pl.ds(i * half, half)],
                target.at[pl.ds(i // 2 * half, half), pl.ds(i % 2 * width, width)], at + i,
            )
            for i in range(4)
        ]

    gate_tiles = weight_tiles(weight_gate_hbm, wide, 6)
    for copy in gate_tiles:
        copy.start()
    scan(1)
    gate_ring.start(1, gate_term)
    scan(2)
    out_hop(2)
    scan(3)
    scan_backward_finish(key_ref, query_ref, key_grad, query_grad, inner_grad)

    for i, ref in ((0, key_grad), (2, query_grad)):
        across = ref[...].T
        for j in (0, 1):
            shared_out[i + j] = across[j * shared : (j + 1) * shared].astype(bf16)

    def shared_copy(k):
        return to_partner(
            k, shared_out.at[partner(k)], shared_in.at[k - 1], swap_send, swap_recv, k - 1
        )

    for k in (2, 3, 1):
        shared_copy(k).start()
    for hop in range(3, far):
        out_hop(hop)
    gate_ring.start(2, gate_term)

    at_row = lax.broadcasted_iota(jnp.int32, (SPAN, SPAN), 0)
    at_lane = lax.broadcasted_iota(jnp.int32, (SPAN, SPAN), 1)
    later = (at_lane >= at_row).astype(f32)
    earlier = (at_lane < at_row).astype(f32)
    rest = precise(
        jnp.concatenate([rest_ref[c] for c in range(chunks)], axis=0), head_pick_ref[...]
    )
    decay, head_mask = heads_ref[0:1, :], heads_ref[1:2, :]
    step_bias_grad = jnp.zeros((1, PAIR), f32)
    decay_grad = jnp.zeros((1, PAIR), f32)
    for c in range(chunks):
        here = slice(c * SPAN, (c + 1) * SPAN)
        sums = sums_ref[here, :]
        log_grad = (
            precise(later, sums)
            + pltpu.roll(precise(earlier, sums), PAIR - heads, 1)
            + rest[c : c + 1]
        )
        steps = pltpu.roll(column_ref[here, :], PAIR - heads, 1)
        logits = pltpu.roll(column_ref[here, :], PAIR - 2 * heads, 1)
        raw_grad = (decay * log_grad + pltpu.roll(sums, PAIR - 2 * heads, 1)) * jax.nn.sigmoid(
            logits
        )
        step_bias_grad = step_bias_grad + jnp.sum(raw_grad, axis=0, keepdims=True)
        decay_grad = decay_grad + jnp.sum(steps * log_grad, axis=0, keepdims=True)
        raw[here, :] = raw_grad * head_mask
    decay_grad = decay_grad * decay

    for k in (2, 3, 1):
        shared_copy(k).wait_recv()
    part, pre = shared_part_ref[...], shared_pre_ref[...]
    gate = jax.nn.sigmoid(pre)
    pre_grad = shared_out[f].astype(f32)
    for k in (1, 2, 3):
        pre_grad = pre_grad + shared_in[k - 1].astype(f32)
    pre_grad = pre_grad * (gate * (1.0 + pre * (1.0 - gate)))
    shared_grad = jnp.zeros_like(pre_grad)
    lane = lax.broadcasted_iota(jnp.int32, (shared, PAIR), 1)
    shared_sums = jnp.where(lane == CONV, jnp.sum(pre_grad, axis=1, keepdims=True), 0.0)
    for k in range(CONV):
        shift = CONV - 1 - k
        shared_grad = shared_grad + taps_ref[:, k : k + 1] * shifted(pre_grad, -shift)
        shared_sums = shared_sums + jnp.where(
            lane == k, jnp.sum(pre_grad * shifted(part, shift), axis=1, keepdims=True), 0.0
        )
    small_t[0:shared, :] = shared_grad.astype(bf16)
    small_t[shared:, :] = raw[...].T[0 : PAIR - shared].astype(bf16)
    small_n[...] = small_t[...].T
    small_ring.start(0, small_term)

    near_copy(0, 0).wait_send()
    tokens_load = load(tokens_hbm, near_out.at[0], 15)
    tokens_load.start()
    near_copy(0, 0).wait_recv()
    near_copy(0, 2).wait_recv()
    tokens_load.wait()
    value = near_out[0].astype(f32) + (
        (kept[...] + near_in[0].astype(f32)) + near_in[2].astype(f32)
    )
    for k in (0, 1):
        pl.semaphore_signal(
            near_free.at[k], inc=1, device_id={"fsdp": partner(k + 1)}, device_id_type=MESH
        )
    for i in (1, 2):
        near_copy(0, i).wait_send()
    near_out[2] = value.astype(bf16)
    layer_store = pltpu.make_async_copy(near_out.at[2], layer_out_hbm, store_sem.at[0])
    layer_store.start()

    for copy in hop_loads(far):
        copy.wait()
    value = out_ring.finish(out_term(far))
    out_raw_ref[...] = jnp.concatenate([value[:rows_out], value[rows_out:]], axis=1)
    squares = total_squares(value)
    for way in (0, 1):
        pl.semaphore_signal(
            ring_free.at[way], inc=1, device_id=ring.target(1 - way), device_id_type=MESH
        )
    x_tiles = weight_tiles(weight_x_hbm, cotangent, 10)
    for copy in x_tiles:
        copy.start()
    for way in (0, 1):
        pl.semaphore_wait(ring_free.at[way], 1)
    x_ring.start(0, x_term)
    for hop in range(3, far):
        gate_ring.start(hop, gate_term)

    for copy in gate_tiles + x_tiles:
        copy.wait()

    def back_block(flip, target, kind):
        here = pl.ds(pl.multiple_of(partner(flip) * tokens, tokens), tokens)
        for i in range(4):
            at = (slice(i // 2 * half, (i // 2 + 1) * half), slice(i % 2 * width, (i % 2 + 1) * width))
            value = (
                dot_lanes(gate_grad[here, :], wide[at])
                + dot_lanes(x_grad[here, :], cotangent[at])
                + dot_lanes(small_n[here, :], weight_small_ref[i * half : (i + 1) * half, :])
            )
            target[:, i * half : (i + 1) * half] = value.astype(kind)

    for k in (0, 1):
        pl.semaphore_wait(near_free.at[k], 1)
    for i, flip in ((1, 3), (0, 1)):
        back_block(flip, near_out.at[i], bf16)
        near_copy(1, i).start()
    small_ring.start(1, small_term)
    back_block(2, kept, f32)
    near_copy(1, 1).wait_recv()
    layer_store.wait()
    near_out[2] = (kept[...] + near_in[1].astype(f32)).astype(bf16)
    near_copy(1, 2).start()
    x_ring.start(1, x_term)
    back_block(0, kept, f32)
    near_copy(1, 1).wait_send()
    own_load = load(cotangent_hbm, near_out.at[1], 14)
    own_load.start()
    near_copy(1, 0).wait_send()
    tokens_load = load(tokens_hbm, near_out.at[0], 15)
    tokens_load.start()

    def return_copy(part, k):
        source = (gate_out, x_out, small_out)[part]
        target = (gate_back, x_back, small_back)[part]
        return to_partner(
            k, row_slice(source, partner(k) * sub, sub), target.at[f],
            return_send, return_recv, part * 3 + k - 1,
        )

    def own_copy(part):
        source = (gate_out, x_out, small_out)[part]
        target = (gate_back, x_back, small_back)[part]
        return pltpu.make_async_copy(
            row_slice(source, f * sub, sub), target.at[f], local_sem.at[part]
        )

    def give_back(part, value):
        (gate_out, x_out, small_out)[part][...] = value.astype(bf16)
        for k in (2, 3, 1):
            return_copy(part, k).start()
        own_copy(part).start()

    value = gate_ring.finish(gate_term)
    squares = squares + total_squares(value)
    give_back(0, value)
    small_ring.start(2, small_term)
    x_ring.start(2, x_term)
    near_copy(1, 0).wait_recv()
    near_copy(1, 2).wait_recv()
    own_load.wait()
    tokens_load.wait()
    inputs = near_out[0].astype(f32)
    inverse = lax.rsqrt(jnp.sum(inputs * inputs, axis=1, keepdims=True) / D + norm_eps)
    normed_grad = (kept[...] + near_in[0].astype(f32)) + near_in[2].astype(f32)
    pulled = normed_grad * norm_gain_row(vectors_own_ref)
    scaled = inputs * inverse
    input_grad = inverse * (
        pulled - scaled * (jnp.sum(pulled * scaled, axis=1, keepdims=True) / D)
    )
    near_out[1] = (near_out[1].astype(f32) + input_grad).astype(bf16)
    token_store = pltpu.make_async_copy(near_out.at[1], token_grad_hbm, store_sem.at[1])
    token_store.start()
    gain_grad = jnp.sum(normed_grad * scaled, axis=0, keepdims=True)

    vector_sum[...] = jnp.zeros_like(vector_sum)
    vector_sum[0:1, :] = gate_gain_ref[0:1, :]
    vector_sum[1 : CONV + 3, :] = channel_ref[0 : CONV + 2, :]
    for i in range(D // width):
        vector_sum[CONV + 3 + i : CONV + 4 + i, :] = gain_grad[:, i * width : (i + 1) * width]
    vector_sum[15:16, 0:PAIR] = step_bias_grad
    vector_sum[15:16, PAIR : 2 * PAIR] = decay_grad
    across = jnp.concatenate([shared_sums, jnp.zeros((PAIR - shared, PAIR), f32)], axis=0)
    vector_sum[16:24, 0:PAIR] = across.T[0:8]

    def vector_copy(step, flip):
        return pltpu.make_async_remote_copy(
            vector_in.at[step, 0], vector_in.at[step, 1], vector_send.at[step],
            vector_recv.at[step],
            device_id={"dp": flipped(d, flip)}, device_id_type=MESH,
        )

    flips = []
    while 1 << len(flips) < count:
        flips.append(1 << len(flips))
    for step, flip in enumerate(flips):
        vector_in[step, 0] = vector_sum[...]
        vector_copy(step, flip).start()
        if step == 0:
            for hop in range(3, far):
                small_ring.start(hop, small_term)
        if step == 1:
            for hop in range(3, far):
                x_ring.start(hop, x_term)
        vector_copy(step, flip).wait_recv()
        vector_sum[...] = vector_sum[...] + vector_in[step, 1]

    def vector_spread(k):
        return to_partner(
            k, vector_sum, vectors_ref.at[f], vector_send, vector_recv, len(flips) + k - 1
        )

    for k in (2, 3, 1):
        vector_spread(k).start()
    vectors_ref[f] = vector_sum[...]

    value = small_ring.finish(small_term)
    squares = squares + total_squares(value)
    give_back(2, value)
    value = x_ring.finish(x_term)
    give_back(1, value)
    squares = squares + total_squares(value)

    total = jnp.broadcast_to(squares, (8, PAIR))
    scalar_out[0] = total

    def near_scalar(k):
        return to_partner(
            k, scalar_out.at[0], scalar_in.at[k], scalar_send, scalar_recv, k
        )

    for k in (2, 3, 1):
        near_scalar(k).start()
    for k in (2, 3, 1):
        near_scalar(k).wait_recv()
    total = (total + scalar_in[1]) + (scalar_in[2] + scalar_in[3])
    scalar_out[1] = total

    def far_scalar(k):
        member = d
        for bit in flips:
            if k & bit:
                member = flipped(member, bit)
        return pltpu.make_async_remote_copy(
            scalar_out.at[1], scalar_in.at[3 + k], scalar_send.at[3 + k], scalar_recv.at[3 + k],
            device_id={"dp": member}, device_id_type=MESH,
        )

    for k in range(count - 1, 0, -1):
        far_scalar(k).start()
    parts = [total]
    for k in range(1, count):
        far_scalar(k).wait_recv()
        parts.append(scalar_in[3 + k])
    while len(parts) > 1:
        parts = [parts[i] + parts[i + 1] for i in range(0, len(parts), 2)]
    total_ref[...] = parts[0]

    for k in (1, 2, 3):
        vector_spread(k).wait_recv()
        vector_spread(k).wait_send()
        shared_copy(k).wait_send()
        near_scalar(k).wait_send()
        for i in range(3):
            return_copy(i, k).wait_recv()
            return_copy(i, k).wait_send()
    for k in range(1, count):
        far_scalar(k).wait_send()
    near_copy(1, 2).wait_send()
    for i in range(3):
        own_copy(i).wait()
    for step, flip in enumerate(flips):
        vector_copy(step, flip).wait_send()
    token_store.wait()


def backward(
    scan_inputs, queries_t, column, heads, shared_part, shared_pre, taps, vectors, gate_gain, tokens,
    weight_small, x, y_grad, states, gated, gated_t, gate_grad, normed_t, cotangents, cotangent,
    weight_out, weight_gate, weight_x,
):
    consts, columns, rows_t, keys, queries = scan_inputs
    length, width = x.shape
    chunks, groups = length // SPAN, width // LANES
    count, members = lax.axis_size("dp"), lax.axis_size("fsdp")
    rows, rows_out = D // count, width // count
    sub, own, shared = rows // members, tokens.shape[0], shared_part.shape[0]
    far = count // 2
    hops = max(count - 1, 1).bit_length()
    assert groups == 4 and count == 8 and members == 4 and 2 * rows_out == rows and 2 * width == D
    head_pick = jnp.asarray(
        (np.arange(width)[:, None] // HEAD_DIM == np.arange(PAIR)[None, :]).astype(np.float32)
    )
    dma, vmem, sd = pltpu.SemaphoreType.DMA, pltpu.VMEM, jax.ShapeDtypeStruct
    return pl.pallas_call(
        backward_kernel,
        in_specs=[whole_spec()] * 16 + any_specs(14),
        out_specs=any_specs(5) + [whole_spec()] * 3,
        out_shape=[
            sd((own, D), bf16),
            sd((own, D), bf16),
            sd((members, sub, width), bf16),
            sd((members, sub, width), bf16),
            sd((members, sub, PAIR), bf16),
            sd((rows_out, D), f32),
            sd((members, 24, width), f32),
            sd((8, PAIR), f32),
        ],
        scratch_shapes=[
            vmem((length, LANES), f32),
            vmem((2, length, LANES), bf16),
            vmem((2, chunks, STATE, LANES), bf16),
            vmem((2, length, PAIR), f32),
            vmem((length + 8, LANES), f32),
            vmem((8, LANES), f32),
            vmem((STATE, LANES), f32),
            vmem((chunks, SPAN, SPAN), f32),
            vmem((length, width), bf16),
            vmem((length, STATE), f32),
            vmem((length, STATE), f32),
            vmem((length, PAIR), f32),
            vmem((chunks, 1, width), f32),
            vmem((8, width), f32),
            vmem((D, length), bf16),
            vmem((length, width), bf16),
            vmem((4, rows_out, length), bf16),
            vmem((length, D), bf16),
            vmem((width, D), bf16),
            vmem((own, D), f32),
            vmem((3, own, D), bf16),
            vmem((3, own, D), bf16),
            vmem((members, shared, length), bf16),
            vmem((members - 1, shared, length), bf16),
            vmem((length, PAIR), f32),
            vmem((PAIR, length), bf16),
            vmem((length, PAIR), bf16),
            vmem((24, width), f32),
            vmem((hops, 2, 24, width), f32),
            vmem((rows, width), bf16),
            vmem((rows, width), bf16),
            vmem((rows, PAIR), bf16),
            vmem((2, 8, PAIR), f32),
            vmem((3 + count, 8, PAIR), f32),
        ]
        + RingScatter.scratch(count, rows, width) * 2
        + RingScatter.scratch(count, rows, PAIR)
        + [
            dma((16,)),
            dma((3, 3)),
            dma((4,)),
            dma((2,)),
            dma((3,)),
            dma((6,)),
            dma((6,)),
            dma((3,)),
            dma((3,)),
            dma((hops + 3,)),
            dma((hops + 3,)),
            dma((9,)),
            dma((9,)),
            dma((3 + count,)),
            dma((3 + count,)),
            dma((4, 2 * far)),
            dma((4, 2 * far)),
            pltpu.SemaphoreType.REGULAR((2,)),
            pltpu.SemaphoreType.REGULAR((2,)),
        ],
        compiler_params=pltpu.CompilerParams(
            collective_id=1, has_side_effects=True, vmem_limit_bytes=BACKWARD_VMEM_BYTES
        ),
        name="backward",
    )(
        rows_t, keys, queries, queries_t, block_mask(), pick_masks(groups), consts, column, heads,
        head_pick, shared_part, shared_pre, taps, vectors, gate_gain, weight_small,
        tokens, x, y_grad, states, columns, gated, gated_t, gate_grad, normed_t, cotangents, cotangent,
        weight_out, weight_gate, weight_x,
    )


OPTIMIZER_STEPS = 4


def optimizer_kernel(
    squares_ref, parts_ref, vector_ref, vector_first_ref, vector_second_ref, turn_ref,
    gate_ref, x_ref, small_ref, in_ref, in_first_ref, in_second_ref,
    out_raw_ref, out_ref, out_first_ref, out_second_ref,
    norm_ref, vector_grad_ref, vector_moment_ref, vector_square_ref, vector_master_ref,
    in_grad_ref, in_moment_ref, in_square_ref, in_master_ref, in_rounded_ref,
    out_grad_ref, out_moment_ref, out_square_ref, out_master_ref, out_rounded_ref,
    joined, factor_ref, in_raw,
):
    members = parts_ref.shape[0]
    pairs = INNER // PAIR
    shared, heads = 2 * STATE // members, HEADS // members

    @pl.when(pl.program_id(0) == 0)
    def _():
        joined[...] = jnp.zeros_like(joined)
        width = parts_ref.shape[2]
        for i in range(D // PAIR):
            row = CONV + 3 + i * PAIR // width
            lanes = slice(i * PAIR % width, i * PAIR % width + PAIR)
            value = parts_ref[0, row : row + 1, lanes]
            for member in range(1, members):
                value = value + parts_ref[member, row : row + 1, lanes]
            joined[i : i + 1, :] = value

        def put_channels(first_row, row):
            for pair in range(pairs):
                at = pair // members
                joined[first_row + pair : first_row + pair + 1, :] = parts_ref[
                    pair % members, row : row + 1, at * PAIR : (at + 1) * PAIR
                ]

        put_channels(D // PAIR, 0)
        each = PAIR // shared
        for k in range(CONV + 1):
            first_row = TAPS_ROW + k * (XBC // PAIR)
            put_channels(first_row, 1 + k)
            for i in range(members // each):
                joined[first_row + pairs + i : first_row + pairs + i + 1, :] = jnp.concatenate(
                    [
                        parts_ref[i * each + j, 16 + k : 17 + k, 0:shared]
                        for j in range(each)
                    ],
                    axis=1,
                )
        precise = partial(jnp.dot, precision=highest, preferred_element_type=f32)
        last, skips = jnp.zeros((1, PAIR), f32), jnp.zeros((1, PAIR), f32)
        local_at = lax.broadcasted_iota(jnp.int32, (PAIR, PAIR), 0)
        head_at = lax.broadcasted_iota(jnp.int32, (PAIR, PAIR), 1)
        channel_head = lax.broadcasted_iota(jnp.int32, (width, PAIR), 0) // HEAD_DIM
        wide_at = lax.broadcasted_iota(jnp.int32, (width, PAIR), 1)
        for member in range(members):
            home = local_at // 2 * 2 * members + 2 * member + local_at % 2
            known = local_at < heads
            biases = parts_ref[member, 15:16, 0:PAIR]
            decays = parts_ref[member, 15:16, PAIR : 2 * PAIR]
            last = last + precise(biases, ((head_at == home) & known).astype(f32))
            last = last + precise(decays, ((head_at == home + HEADS) & known).astype(f32))
            home = channel_head // 2 * 2 * members + 2 * member + channel_head % 2
            skips = skips + precise(
                parts_ref[member, CONV + 2 : CONV + 3, :], (wide_at == home).astype(f32)
            )
        joined[LAST_ROW : LAST_ROW + 1, :] = last
        joined[LAST_ROW + 1 : LAST_ROW + 2, :] = skips
        vector_raw = joined[...]
        norm = jnp.sqrt(squares_ref[...] + total_squares(vector_raw))
        norm_ref[...] = norm
        factor = jnp.minimum(1.0, clip_norm / (norm + 1e-06))
        factor_ref[...] = factor
        grad = vector_raw * factor[0:1, 0:1]
        vector_grad_ref[...] = grad
        vector_moment_ref[...], vector_square_ref[...], vector_master_ref[...] = adamw(
            vector_ref[...], vector_first_ref[...], vector_second_ref[...], grad, rate_vectors
        )

    factor = factor_ref[0:1, 0:1]
    for pair in range(pairs):
        at = pair // members
        lanes, held = slice(pair * PAIR, (pair + 1) * PAIR), slice(at * PAIR, (at + 1) * PAIR)
        in_raw[:, lanes] = gate_ref[pair % members, :, held].astype(f32)
        in_raw[:, INNER + pair * PAIR : INNER + (pair + 1) * PAIR] = x_ref[
            pair % members, :, held
        ].astype(f32)
    small = jnp.concatenate([small_ref[i] for i in range(members)], axis=1)
    in_raw[:, 2 * INNER :] = dot_rows(small, turn_ref[...])
    grad = in_raw[...] * factor
    in_grad_ref[...] = grad
    in_moment_ref[...], in_square_ref[...], master = adamw(
        in_ref[...], in_first_ref[...], in_second_ref[...], grad, rate_in_proj
    )
    in_master_ref[...] = master
    in_rounded_ref[...] = master.astype(bf16)
    grad = out_raw_ref[...] * factor
    out_grad_ref[...] = grad
    out_moment_ref[...], out_square_ref[...], master = adamw(
        out_ref[...], out_first_ref[...], out_second_ref[...], grad, rate_out_proj
    )
    out_master_ref[...] = master
    out_rounded_ref[...] = master.astype(bf16)


def optimizer(squares, parts, vectors, gate, x, small, in_state, out_raw, out_state):
    members, rows, width = x.shape
    in_shape, out_shape = in_state[0].shape, out_state[0].shape
    steps = OPTIMIZER_STEPS
    step_rows = rows // steps
    piece = lambda lanes: pl.BlockSpec((members, step_rows, lanes), lambda i: (0, i, 0))
    in_flat = pl.BlockSpec((step_rows, in_shape[1]), lambda i: (i, 0))
    out_flat = pl.BlockSpec((out_shape[0] // steps, out_shape[1]), lambda i: (i, 0))
    sd = jax.ShapeDtypeStruct
    vector_shape = sd(vectors[0].shape, f32)
    return pl.pallas_call(
        optimizer_kernel,
        grid=(steps,),
        in_specs=[whole_spec()] * 6
        + [piece(width), piece(width), piece(PAIR)]
        + [in_flat] * 3
        + [out_flat] * 4,
        out_specs=[whole_spec()] * 5 + [in_flat] * 5 + [out_flat] * 5,
        out_shape=[sd((8, PAIR), f32)]
        + [vector_shape] * 4
        + [sd(in_shape, f32)] * 4
        + [sd(in_shape, bf16)]
        + [sd(out_shape, f32)] * 4
        + [sd(out_shape, bf16)],
        scratch_shapes=[
            pltpu.VMEM(vectors[0].shape, f32),
            pltpu.VMEM((8, PAIR), f32),
            pltpu.VMEM((step_rows, in_shape[1]), f32),
        ],
        compiler_params=pltpu.CompilerParams(vmem_limit_bytes=VMEM_BYTES),
        name="optimizer",
    )(
        squares, parts, *vectors, last_columns(members), gate, x, small, *in_state, out_raw,
        *out_state,
    )


def unpack(vectors):
    offset = D + INNER
    taps_end = offset + CONV * XBC
    heads_start = taps_end + XBC
    norm_gain = vectors[:D]
    gate_gain = vectors[D:offset]
    filter_taps = vectors[offset:taps_end].reshape(CONV, XBC)
    filter_bias = vectors[taps_end:heads_start]
    step_bias = vectors[heads_start : heads_start + HEADS]
    decay_log = vectors[heads_start + HEADS : heads_start + 2 * HEADS]
    skip_gain = vectors[heads_start + 2 * HEADS : heads_start + 3 * HEADS]
    return (norm_gain, gate_gain, filter_taps, filter_bias, step_bias, decay_log, skip_gain)


def adamw(weight, moment, square, gradient, step_rate):
    moment_new = beta_first * moment + (1.0 - beta_first) * gradient
    square_new = beta_second * square + (1.0 - beta_second) * gradient * gradient
    moment_hat = moment_new / (1.0 - beta_first**STEP)
    square_hat = square_new / (1.0 - beta_second**STEP)
    weight_new = weight - step_rate * (
        moment_hat / (jnp.sqrt(square_hat) + adam_eps) + weight_decay * weight
    )
    return (moment_new, square_new, weight_new)


def on_device(
    tokens,
    widths,
    cotangent,
    in_weight,
    in_first,
    in_second,
    out_weight,
    out_first,
    out_second,
    vectors,
    vector_first,
    vector_second,
):
    fsdp = lax.axis_size("fsdp")
    me = lax.axis_index("fsdp")
    heads = HEADS // fsdp
    inner = INNER // fsdp
    shared = 2 * STATE // fsdp
    pairs = HEADS // 2 // fsdp
    rows_in, rows_out = in_weight.shape[0], out_weight.shape[0]
    length = tokens.shape[0] * fsdp
    chunks = length // SPAN
    in_kernels = uses_ring("dp") and rows_out == PAIR and rows_in % 16 == 0

    def own_channels(v):
        lead = v.shape[:-1]
        cut = v.reshape(lead + (pairs, fsdp, PAIR))
        return lax.dynamic_index_in_dim(cut, me, len(lead) + 1, False).reshape(lead + (inner,))

    def own_heads(v):
        return lax.dynamic_index_in_dim(v.reshape(pairs, fsdp, 2), me, 1, False).reshape(heads)

    def own_shared(v):
        return lax.dynamic_slice_in_dim(v, me * shared, shared, v.ndim - 1)

    norm_gain, gate_gain, filter_taps, filter_bias, step_bias, decay_log, skip_gain = unpack(
        vectors
    )
    gain_own = own_channels(gate_gain)[None]
    taps_own = own_channels(filter_taps[:, :INNER])
    bias_own = own_channels(filter_bias[:INNER])[None]
    taps_shared = own_shared(filter_taps[:, INNER:])
    bias_shared = own_shared(filter_bias[INNER:])
    step_bias_own, decay_own = own_heads(step_bias), -jnp.exp(own_heads(decay_log))
    skip_own = jnp.repeat(own_heads(skip_gain), HEAD_DIM)[None]

    width_index = widths[0]
    active = HEADS // 8 * jnp.left_shift(jnp.int32(1), width_index)
    head_mask = (jnp.arange(heads, dtype=jnp.int32) < active // fsdp).astype(f32)
    mask = jnp.repeat(head_mask, HEAD_DIM)[None]
    channel_count = (active * HEAD_DIM).astype(f32)

    inputs = tokens.astype(f32)
    inverse_in = lax.rsqrt(jnp.mean(inputs * inputs, axis=-1, keepdims=True) + norm_eps)

    if in_kernels:
        vector_state = [vector_tiles(v) for v in (vectors, vector_first, vector_second)]
        (
            weight_shared, weight_x, weight_gate, weight_out, cotangents, normed_t, x_part, states,
            gated_low, gated_t, y_grad, gate_grad, consts, head_consts, shared_taps, head_columns,
            head_rows, head_all, keys, queries, queries_t, shared_part, shared_pre, gain_grad,
        ) = forward(tokens, cotangent, in_weight, out_weight, vector_state[0], active)
        scan_inputs = (consts, head_columns, head_rows, keys, queries)
    else:
        in_low = in_weight.astype(bf16)
        shared_cut = jnp.concatenate(
            [
                in_low[:, 2 * INNER : 2 * INNER + 2 * STATE]
                .reshape(rows_in, fsdp, shared)
                .transpose(1, 0, 2),
                in_low[:, 2 * INNER + 2 * STATE :]
                .reshape(rows_in, pairs, fsdp, 2)
                .transpose(2, 0, 1, 3)
                .reshape(fsdp, rows_in, heads),
            ],
            axis=2,
        )

        def channel_cut(part):
            return (
                part.reshape(rows_in, pairs, fsdp, PAIR)
                .transpose(2, 0, 1, 3)
                .reshape(fsdp, rows_in, inner)
            )

        def gathered(cut):
            block = exchanged(cut, "fsdp")
            return gather_rows(block.reshape(fsdp * rows_in, cut.shape[2]), "dp")

        normed_own = (inputs * inverse_in * norm_gain[None, :]).astype(bf16)
        x_cut = channel_cut(in_low[:, INNER : 2 * INNER])
        gate_cut = channel_cut(in_low[:, :INNER])
        out_low = out_weight.astype(bf16)

        weight_shared = gathered(shared_cut)
        weight_x = gathered(x_cut)
        weight_gate = gathered(gate_cut)
        weight_out = lax.dynamic_index_in_dim(
            lax.all_gather(out_low, ("dp", "fsdp"), axis=0, tiled=True).reshape(
                pairs, fsdp, PAIR, D
            ),
            me,
            1,
            False,
        ).reshape(inner, D)
        normed = spread(normed_own, "fsdp").reshape(length, D)
        cotangents = spread(cotangent, "fsdp").reshape(length, D)

        small = lax.dot_general(
            weight_shared, normed, (((0,), (1,)), ((), ())), preferred_element_type=f32
        )
        shared_part = small[:shared]
        step_raw = small[shared : shared + heads] * head_mask[:, None]
        shared_padded = jnp.pad(shared_part, ((0, 0), (CONV - 1, 0)))
        shared_pre = bias_shared[:, None] + sum(
            taps_shared[k][:, None] * shared_padded[:, k : k + length] for k in range(CONV)
        )
        shared_gate = jax.nn.sigmoid(shared_pre)
        shared_all = spread_small((shared_pre * shared_gate).astype(bf16), "fsdp").reshape(
            2 * STATE, length
        )
        keys_t, queries_t = shared_all[:STATE], shared_all[STATE:]
        keys, queries = keys_t.T, queries_t.T
        step_logits = step_raw + step_bias_own[:, None]
        step_sizes = jax.nn.softplus(step_logits)
        upto = (jnp.arange(SPAN)[:, None] <= jnp.arange(SPAN)[None, :]).astype(f32)
        log_sums = jnp.dot(
            (step_sizes * decay_own[:, None]).reshape(heads, chunks, SPAN), upto, precision=highest
        ).reshape(heads, length)
        groups = heads // GROUP
        head_all = jnp.concatenate(
            [log_sums, step_sizes, step_logits, jnp.zeros((PAIR - 3 * heads, length), f32)]
        ).T
        head_columns = jnp.concatenate(
            [jnp.roll(head_all, -group * GROUP, axis=1) for group in range(groups)], axis=1
        )
        head_rows = jnp.pad(
            log_sums.reshape(groups, GROUP, length), ((0, 0), (0, 8 - GROUP), (0, 0))
        ).reshape(groups * 8, length)

        consts = jnp.concatenate([taps_own, bias_own, mask, skip_own, gain_own])
        scan_inputs = (consts, head_columns, head_rows, keys, queries)
        x_part = jnp.dot(normed, weight_x, preferred_element_type=f32)
        y, states = scan_forward(x_part, *scan_inputs, keys_t)
        gate_part, gated_grad, stats = gate_forward(
            normed, weight_gate, cotangents, weight_out, y, gain_own, mask
        )
        stats = summed(stats[:, :2].T, "fsdp")
        inverse_out = lax.rsqrt(stats[0] / channel_count + norm_eps)
        pull = inverse_out**3 / channel_count * stats[1]
        gated_low, y_grad, gate_grad, gain_grad = norm_back(
            y, gate_part, gated_grad, jnp.stack([inverse_out, pull], axis=1), gain_own, mask
        )

        def in_term(grad):
            return lax.dot_general(
                normed, grad, (((0,), (0,)), ((), ())), preferred_element_type=f32
            ).astype(bf16)

    if in_kernels:
        (
            layer_out, token_grad, gate_back, x_back, small_back, out_raw, vector_rows, squares,
        ) = backward(
            scan_inputs, queries_t, head_all, head_consts, shared_part, shared_pre, shared_taps,
            vector_state[0], gain_grad, tokens, weight_shared, x_part, y_grad, states, gated_low,
            gated_t, gate_grad, normed_t, cotangents, cotangent, weight_out, weight_gate, weight_x,
        )
        norm, *rest = optimizer(
            squares, vector_rows, vector_state, gate_back, x_back, small_back,
            (in_weight, in_first, in_second), out_raw, (out_weight, out_first, out_second),
        )
        vector_out = [v.reshape(-1)[: vectors.shape[0]] for v in rest[:4]]
        in_grad, in_moment, in_square, in_master, in_rounded = rest[4:9]
        out_grad, out_moment, out_square, out_master, out_rounded = rest[9:]
        return (
            layer_out,
            token_grad,
            in_grad,
            out_grad,
            vector_out[0],
            norm[0, 0],
            in_moment,
            in_square,
            in_master,
            in_rounded,
            out_moment,
            out_square,
            out_master,
            out_rounded,
            *vector_out[1:],
        )
    else:
        out_term = lax.dot_general(
            gated_low, cotangents, (((0,), (0,)), ((), ())), preferred_element_type=f32
        )
        whole_term = jnp.zeros((pairs, fsdp, PAIR, D), f32)
        whole_term = lax.dynamic_update_slice(
            whole_term, out_term.reshape(pairs, 1, PAIR, D), (0, me, 0, 0)
        )
        out_raw = lax.psum_scatter(
            whole_term.reshape(INNER, D), ("dp", "fsdp"), scatter_dimension=0, tiled=True
        )
        added = halved(
            jnp.dot(gated_low, weight_out, preferred_element_type=f32)
            .astype(bf16)
            .reshape(fsdp, tokens.shape[0], D),
            "fsdp",
        )
        layer_out = (inputs + added).astype(bf16)
        gate_raw = scatter_rows(in_term(gate_grad), "dp")
        x_grad, key_grad, query_grad, sums, rest, channel_grad = scan_backward(
            x_part, *scan_inputs, queries_t, y_grad, states
        )
        x_raw = scatter_rows(in_term(x_grad), "dp")

        shared_grads = jnp.concatenate([key_grad, query_grad], axis=1).T.astype(bf16)
        arrived = exchanged(shared_grads.reshape(fsdp, shared, length), "fsdp").astype(f32)
        activated_grad = jnp.sum(arrived, axis=0)
        shared_pre_grad = activated_grad * shared_gate * (1.0 + shared_pre * (1.0 - shared_gate))
        shared_ahead = jnp.pad(shared_pre_grad, ((0, 0), (0, CONV - 1)))
        shared_grad = sum(
            taps_shared[k][:, None] * shared_ahead[:, CONV - 1 - k : CONV - 1 - k + length]
            for k in range(CONV)
        )
        taps_shared_grad = jnp.stack(
            [
                jnp.sum(shared_pre_grad * shared_padded[:, k : k + length], axis=1)
                for k in range(CONV)
            ]
        )
        bias_shared_grad = jnp.sum(shared_pre_grad, axis=1)

        sums = sums.T[: 3 * heads].reshape(3, heads, chunks, SPAN)
        before = (jnp.arange(SPAN)[:, None] < jnp.arange(SPAN)[None, :]).astype(f32)
        rest = rest.reshape(chunks, heads, HEAD_DIM).sum(axis=2).T
        log_grad = (
            jnp.dot(sums[0], 1.0 - before, precision=highest)
            + jnp.dot(sums[1], before, precision=highest)
            + rest[:, :, None]
        ).reshape(heads, length)
        step_grad = decay_own[:, None] * log_grad + sums[2].reshape(heads, length)
        raw_grad = step_grad * jax.nn.sigmoid(step_logits)
        step_bias_grad = jnp.sum(raw_grad, axis=1)
        decay_grad = jnp.sum(step_sizes * log_grad, axis=1) * decay_own
        small_grad = jnp.concatenate([shared_grad, raw_grad * head_mask[:, None]], axis=0).astype(bf16)
        small_raw = scatter_rows(
            lax.dot_general(
                normed, small_grad, (((0,), (1,)), ((), ())), preferred_element_type=f32
            ).astype(bf16),
            "dp",
        )

        def in_back(grad, weight, grad_dim=1):
            return lax.dot_general(
                grad, weight, (((grad_dim,), (1,)), ((), ())), preferred_element_type=f32
            )

        normed_grad = halved(
            (
                in_back(gate_grad, weight_gate)
                + in_back(x_grad, weight_x)
                + in_back(small_grad, weight_shared, 0)
            )
            .astype(bf16)
            .reshape(fsdp, tokens.shape[0], D),
            "fsdp",
        )
        pulled = normed_grad * norm_gain[None, :]
        input_grad = inverse_in * pulled - inputs * (
            inverse_in**3 * jnp.mean(pulled * inputs, axis=-1, keepdims=True)
        )
        token_grad = (cotangent.astype(f32) + input_grad).astype(bf16)
        norm_gain_grad = jnp.sum(normed_grad * inputs * inverse_in, axis=0)

        head_row = jnp.concatenate(
            [jnp.pad(step_bias_grad, (0, PAIR - heads)), jnp.pad(decay_grad, (0, PAIR - heads))]
        )
        shared_rows = jnp.concatenate([taps_shared_grad, bias_shared_grad[None]])
        vector_rows = jnp.concatenate(
            [
                gain_grad[0:1],
                channel_grad[: CONV + 2],
                norm_gain_grad.reshape(-1, inner),
                jnp.zeros((15 - CONV - 3 - D // inner, inner), f32),
                jnp.pad(head_row, (0, inner - 2 * PAIR))[None],
                jnp.pad(shared_rows, ((0, 7 - CONV), (0, inner - shared))),
            ]
        )
        vector_rows = spread_small(summed_in_steps(vector_rows, "dp"), "fsdp")
        squares = (
            jnp.sum(gate_raw * gate_raw)
            + jnp.sum(x_raw * x_raw)
            + jnp.sum(small_raw * small_raw)
            + jnp.sum(out_raw * out_raw)
        )
        squares = summed(summed(jnp.broadcast_to(squares, (8, 128)), "fsdp"), "dp")[0, 0]

    def joined_channels(v):
        return v.reshape(fsdp, pairs, PAIR).transpose(1, 0, 2).reshape(INNER)

    def joined_heads(v):
        return v.reshape(fsdp, pairs, 2).transpose(1, 0, 2).reshape(HEADS)

    shared_all = vector_rows[:, 16 : 17 + CONV, :shared]
    bias_shared_all = shared_all[:, CONV].reshape(-1)
    taps_all = [
        jnp.concatenate([joined_channels(vector_rows[:, 1 + k]), shared_all[:, k].reshape(-1)])
        for k in range(CONV)
    ]
    bias_all = jnp.concatenate([joined_channels(vector_rows[:, CONV + 1]), bias_shared_all])
    norm_rows = vector_rows[:, CONV + 3 : CONV + 3 + D // inner].reshape(fsdp, D)
    norm_all = norm_rows[0]
    for member in range(1, fsdp):
        norm_all = norm_all + norm_rows[member]
    skip_all = vector_rows[:, CONV + 2].reshape(fsdp * heads, HEAD_DIM).sum(axis=1)
    vector_raw = jnp.concatenate(
        [norm_all, joined_channels(vector_rows[:, 0])]
        + taps_all
        + [
            bias_all,
            joined_heads(vector_rows[:, 15, :heads]),
            joined_heads(vector_rows[:, 15, PAIR : PAIR + heads]),
            joined_heads(skip_all),
        ]
    )

    grad_norm = jnp.sqrt(squares + jnp.sum(vector_raw * vector_raw))
    factor = jnp.minimum(1.0, clip_norm / (grad_norm + 1e-06))
    def returned(raw):
        return exchanged(raw.astype(bf16).reshape(fsdp, rows_in, raw.shape[1]), "fsdp")

    def joined_columns(part):
        return (
            part.reshape(fsdp, rows_in, pairs, PAIR)
            .transpose(1, 2, 0, 3)
            .reshape(rows_in, INNER)
        )

    small_back = returned(small_raw)
    in_raw = jnp.concatenate(
        [
            joined_columns(returned(gate_raw)),
            joined_columns(returned(x_raw)),
            small_back[:, :, :shared].transpose(1, 0, 2).reshape(rows_in, 2 * STATE),
            small_back[:, :, shared:]
            .reshape(fsdp, rows_in, pairs, 2)
            .transpose(1, 2, 0, 3)
            .reshape(rows_in, HEADS),
        ],
        axis=1,
    ).astype(f32)
    in_grad = in_raw * factor
    in_moment, in_square, in_master = adamw(
        in_weight, in_first, in_second, in_grad, rate_in_proj
    )
    in_rounded = in_master.astype(bf16)
    out_grad = out_raw * factor
    vector_grad = vector_raw * factor
    out_moment, out_square, out_master = adamw(
        out_weight, out_first, out_second, out_grad, rate_out_proj
    )
    vector_moment, vector_square, vector_master = adamw(
        vectors, vector_first, vector_second, vector_grad, rate_vectors
    )
    return (
        layer_out,
        token_grad,
        in_grad,
        out_grad,
        vector_grad,
        grad_norm,
        in_moment,
        in_square,
        in_master,
        in_rounded,
        out_moment,
        out_square,
        out_master,
        out_master.astype(bf16),
        vector_moment,
        vector_square,
        vector_master,
    )


def solution(mesh):
    rows = P(("dp", "fsdp"), None)
    return jax.shard_map(
        on_device,
        mesh=mesh,
        in_specs=(rows, P("dp")) + (rows,) * 7 + (P(),) * 3,
        out_specs=(rows,) * 4 + (P(),) * 2 + (rows,) * 8 + (P(),) * 3,
        check_vma=False,
    )
```

profile of v0, /device:TPU:0, one launch (start us, length us, event | category | flops | bytes accessed | tf_op | source)
XLA Modules:
  0.0 354.8 jit_solution(17195312861232233787)
XLA Ops:
  0.7 1.6 pad_bitcast_fusion.2.vectors_ref.vectors_own_ref.vector_ref
  2.9 0.6 broadcast_in_dim.3.active_ref
  3.5 175.7 %forward.1 = (bf16[2048,128]{1,0:T(8,128)(2,1)}, bf16[2048,1024]{1,0:T(8,128)(2,1)}, bf16[2048,1024]{1,0:T(8,128)(2,1)}, bf16[1024,2048]{1,0:T(8,128)(2,1)}, bf1...) custom-call(bf16[256,2048]{1,0:T(8,128)(2,1)} %tokens_hbm.1, ...), custom_call_target="tpu_custom_call" | custom-call | tf_op jit(solution)/shard_map/forward/pallas_call | solution.py:1213
  179.1 0.0 copy-start.2
  179.1 0.0 copy-start.3
  179.1 158.4 %backward.1 = (bf16[256,2048]{1,0:T(8,128)(2,1)}, bf16[256,2048]{1,0:T(8,128)(2,1)}, bf16[4,64,1024]{2,1,0:T(8,128)(2,1)}, bf16[4,64,1024]{2,1,0:T(8,128)(2,1)},...) custom-call(f32[32,1024]{1,0:T(8,128)} %get-tuple-element.64.rows_ref, ...), custom_call_target="tpu_custom_call" | custom-call | tf_op jit(solution)/shard_map/backward/pallas_call | solution.py:1808
  337.5 0.0 copy-done.2
  337.5 0.0 copy-done.3
  337.5 0.7 pad_bitcast_fusion
  338.2 0.0 copy-start.1
  338.2 13.1 %optimizer.1 = (f32[8,128]{1,0:T(8,128)}, f32[220,128]{1,0:T(8,128)}, f32[220,128]{1,0:T(8,128)}, f32[220,128]{1,0:T(8,128)}, f32[220,128]{1,0:T(8,128)}, /*inde...) custom-call(f32[8,128]{1,0:T(8,128)} %get-tuple-element.90.squares_r, ...), custom_call_target="tpu_custom_call" | custom-call | tf_op jit(solution)/shard_map/optimizer/pallas_call | solution.py:2007
  351.3 0.0 copy-start
  351.3 1.3 slice.16
  352.6 0.0 copy-done.1
  352.6 1.0 copy.38
  353.6 0.0 copy-done
  353.6 1.0 copy.39
Async XLA Ops:
  179.1 158.4 %copy-start.2 = (f32[28096]{0:T(1024)S(1)}, f32[28096]{0:T(1024)}, u32[]{:S(2)}) copy-start(f32[28096]{0:T(1024)} %param.29) | copy-start | bytes 337156
  179.1 158.4 %copy-start.3 = (f32[28096]{0:T(1024)S(1)}, f32[28096]{0:T(1024)}, u32[]{:S(2)}) copy-start(f32[28096]{0:T(1024)} %param.28) | copy-start | bytes 337156
  338.2 14.4 %copy-start.1 = (bf16[256,2048]{1,0:T(8,128)(2,1)S(1)}, bf16[256,2048]{1,0:T(8,128)(2,1)}, u32[]{:S(2)}) copy-start(bf16[256,2048]{1,0:T(8,128)(2,1)} %get-tuple-element.130) | copy-start | bytes 3145732
  351.3 2.3 copy-start
where the time goes:
time: 358 us; the launch traced here: 355 us
  Pallas kernels  347 us (97%)
  local copies, waits for them, and re-layouts  6.08 us (2%)
    pallas_call x1, Pallas kernels, forward(): pl.pallas_call(forward_kernel, in_specs=[whole_spec()] + any_specs(1) + [...  176 us
    pallas_call x1, Pallas kernels, backward(): pl.pallas_call(backward_kernel, in_specs=[whole_spec()] * 16 + any_specs(...  158 us
    pallas_call x1, Pallas kernels, optimizer(): pl.pallas_call(optimizer_kernel, grid=(steps,), in_specs=[whole_spec()] *...  13.1 us

commit v1 on v0

--- a/solution.py
+++ b/solution.py
@@ -39,8 +39,7 @@
 highest = lax.Precision.HIGHEST
 f32 = jnp.float32
 bf16 = jnp.bfloat16
-VMEM_BYTES = 60 * 1024 * 1024
-BACKWARD_VMEM_BYTES = 63 * 1024 * 1024
+VMEM_BYTES = 63 * 1024 * 1024
 
 
 def ring_order(count):
@@ -666,8 +665,9 @@
 
 
 class RingGather:
-    def __init__(self, ring, wholes, send, recv):
+    def __init__(self, ring, wholes, send, recv, first):
         self.ring, self.wholes, self.send, self.recv = ring, wholes, send, recv
+        self.first = first
 
     @staticmethod
     def semaphores(parts, count):
@@ -680,8 +680,11 @@
         owner = self.ring.member(-hop if way == 0 else hop)
         place = row_slice(whole, owner * rows + half * size, size)
         at = ((part * 2 + way) * 2 + half) * self.ring.far + hop
+        source = place
+        if hop == 0 and part in self.first:
+            source = row_slice(self.first[part], half * size, size)
         return pltpu.make_async_remote_copy(
-            place, place, self.send.at[at], self.recv.at[at],
+            source, place, self.send.at[at], self.recv.at[at],
             device_id=self.ring.target(way), device_id_type=MESH,
         )
 
@@ -699,12 +702,15 @@
                 self.copy(part, way, half, hop - 1).wait_recv()
             self.copy(part, way, half, hop).start()
 
+    def settle(self, part):
+        last = self.ring.far - 1
+        for way, half in self.pieces(last):
+            self.copy(part, way, 1 - half, last - 1).wait_recv()
+
     def finish(self, part):
         last = self.ring.far - 1
         for way, half in self.pieces(last):
             self.copy(part, way, half, last).wait_recv()
-            if last:
-                self.copy(part, way, 1 - half, last - 1).wait_recv()
         for hop in range(last + 1):
             for way, half in self.pieces(hop):
                 self.copy(part, way, half, hop).wait_send()
@@ -810,10 +816,10 @@
     consts_ref, head_ref, shared_taps_ref, columns_ref, rows_ref, column_ref, keys_ref, queries_ref, queries_t_ref,
     shared_part_ref, shared_pre_ref, gain_grad_ref,
     small_cut, x_cut, gate_cut, out_low, normed, cotangent, small_weight, keys_t, shared_all,
-    x_part, states, y, gate_part, gated_grad, weight, out_tile, turned, squares, products, stats, stats_in,
+    x_part, states, y, gate_part, gated_grad, weight, gate_weight, far_weight, out_tile, turned, squares, products, stats, stats_in,
     back_tiles, back_tiles_t, padded, state, shared_wide,
     local_sem, swap_send, swap_recv, token_send, token_recv, ring_send, ring_recv,
-    shared_send, shared_recv, stats_send, stats_recv, load_sem, store_sem,
+    shared_send, shared_recv, stats_send, stats_recv, load_sem, gate_sem, store_sem,
 ):
     ring = Ring()
     d, f = ring.me, lax.axis_index("fsdp")
@@ -826,7 +832,7 @@
     greet([{"fsdp": partner(k)} for k in (1, 2, 3)] + [ring.target(0), ring.target(1)])
     wholes = [small_all, x_all, gate_all, out_all]
     small_part, x_of, gate_of, out_of = range(4)
-    rings = RingGather(ring, wholes, ring_send, ring_recv)
+    rings = RingGather(ring, wholes, ring_send, ring_recv, {out_of: out_low})
     cuts = [small_cut, x_cut, gate_cut]
 
     def own_copy(part):
@@ -850,8 +856,8 @@
         own_copy(part).start()
 
     def start_ring(part):
-        own_copy(part).wait()
         if part != out_of:
+            own_copy(part).wait()
             for k in (1, 2, 3):
                 swap(part, k).wait_recv()
         rings.start(part, 0)
@@ -865,13 +871,13 @@
 
     out_low[...] = out_ref[...].astype(bf16)
     own_copy(out_of).start()
+    start_ring(out_of)
     pieces = dot_lanes(in_ref[:, 2 * INNER :].astype(bf16), turn_ref[...]).astype(bf16)
     for member in range(4):
         small_cut[member] = pieces[:, member * PAIR : (member + 1) * PAIR]
     start_swaps(small_part)
     cut_channels(x_cut, INNER)
     start_swaps(x_of)
-    start_ring(out_of)
     inputs = tokens_ref[...].astype(f32)
     inverse = lax.rsqrt(jnp.sum(inputs * inputs, axis=1, keepdims=True) / D + norm_eps)
     own_rows = pl.ds(pl.multiple_of(f * tokens, tokens), tokens)
@@ -932,15 +938,16 @@
     ).T
     shared_taps_ref[...] = shared_wide[pl.ds(pl.multiple_of(f % 2 * shared, shared), shared), :]
     rings.start(small_part, 1)
+    rings.start(out_of, 1)
     rings.start(small_part, 2)
     rings.start(x_of, 1)
-    rings.start(out_of, 1)
     for hop in range(3, ring.far):
         rings.start(small_part, hop)
     normed_copies[0].wait_recv()
     normed_copies[2].start()
     for copy in cotangent_copies[:2]:
         copy.start()
+    rings.settle(small_part)
     rings.finish(small_part)
     load_small = pltpu.make_async_copy(small_all, small_weight, local_sem.at[5])
     load_small.start()
@@ -965,8 +972,8 @@
 
     for k in (2, 3, 1):
         shared_copy(k).start()
+    rings.start(out_of, 2)
     rings.start(x_of, 2)
-    rings.start(out_of, 2)
     head_columns = jnp.concatenate(
         [head_ref[...], jnp.zeros((PAIR - 8, PAIR), f32)], axis=0
     ).T[0:heads]
@@ -1005,8 +1012,9 @@
     keys_ref[...] = keys_t[...].T
     queries_ref[...] = queries_t_ref[...].T
     for hop in range(3, ring.far):
+        rings.start(out_of, hop)
         rings.start(x_of, hop)
-        rings.start(out_of, hop)
+    start_ring(gate_of)
     cotangent_copies[0].wait_recv()
     cotangent_copies[2].start()
 
@@ -1023,8 +1031,25 @@
             turned_store(i - 2).wait()
         turned[i % 2] = normed[:, i * quarter : (i + 1) * quarter].T
         turned_store(i).start()
+    rings.settle(x_of)
     rings.finish(x_of)
-    start_ring(gate_of)
+
+    def gate_load(distance, slot):
+        owner = ring.member(distance)
+        size = 4 * sub
+        return pltpu.make_async_copy(
+            row_slice(gate_all, owner * size, size), row_slice(gate_weight, owner * size, size),
+            gate_sem.at[slot],
+        )
+
+    def start_gate(hop):
+        rings.start(gate_of, hop)
+        if hop == ring.far - 1:
+            rings.settle(gate_of)
+        if hop == 1:
+            gate_load(0, 0).start()
+        gate_load(-hop, 2 * hop - 1).start()
+        gate_load(hop, 2 * hop).start()
 
     def lanes(group):
         return pl.ds(group * LANES, LANES)
@@ -1059,14 +1084,16 @@
         )
         states_store(group).start()
         if group % 2 == 1 and group // 2 + 1 < ring.far - 1:
-            rings.start(gate_of, group // 2 + 1)
+            start_gate(group // 2 + 1)
 
     for copy in cotangent_copies[1:]:
         copy.wait_recv()
     cotangent_own.wait()
     cotangent_store = store(cotangent, cotangent_all, 12)
     cotangent_store.start()
+    rings.settle(out_of)
     rings.finish(out_of)
+    own_copy(out_of).wait()
 
     def load_rows(group):
         return pltpu.make_async_copy(
@@ -1079,19 +1106,29 @@
             load_rows(group + 1).start()
         load_rows(group).wait()
         gated_grad[:, lanes(group)] = dot_lanes(cotangent[...], out_tile[group % 2])
-    rings.start(gate_of, ring.far - 1)
+    start_gate(ring.far - 1)
+    far_size = 4 * sub
+    far_rows = pl.ds(pl.multiple_of(ring.member(ring.far) * far_size, far_size), far_size)
+    gate_weight[far_rows, :] = jnp.zeros((far_size, width), bf16)
+    for hop in range(1, ring.far):
+        if hop == 1:
+            gate_load(0, 0).wait()
+        gate_load(-hop, 2 * hop - 1).wait()
+        gate_load(hop, 2 * hop).wait()
+    for group in range(groups):
+        gate_part[:, lanes(group)] = dot_rows(normed[...], gate_weight[:, lanes(group)])
     rings.finish(gate_of)
 
     def const_row(row, here):
         return consts_ref[row : row + 1, here]
 
-    load_columns(gate_all, 0).start()
+    far_load = pltpu.make_async_copy(gate_all.at[far_rows], far_weight, gate_sem.at[7])
+    far_load.start()
+    far_load.wait()
     for group in range(groups):
-        if group + 1 < groups:
-            load_columns(gate_all, group + 1).start()
-        load_columns(gate_all, group).wait()
         here = lanes(group)
-        value = dot_rows(normed[...], weight[group % 2]) * const_row(MASK_ROW, here)
+        value = gate_part[:, here] + dot_rows(normed[:, far_rows], far_weight[:, here])
+        value = value * const_row(MASK_ROW, here)
         gate_part[:, here] = value
         gated = y[:, here] * (value * jax.nn.sigmoid(value))
         product = gated * (gated_grad[:, here] * const_row(GAIN_ROW, here))
@@ -1256,6 +1293,8 @@
             vmem((length, inner), f32),
             vmem((length, inner), f32),
             vmem((2, D, LANES), bf16),
+            vmem((D, inner), bf16),
+            vmem((D // count, inner), bf16),
             vmem((2, LANES, D), bf16),
             vmem((2, D // 4, length), bf16),
             vmem((length, PAIR), f32),
@@ -1279,6 +1318,7 @@
             dma((3,)),
             dma((3,)),
             dma((4,)),
+            dma((8,)),
             dma((13 + 4 * groups,)),
         ],
         compiler_params=pltpu.CompilerParams(
@@ -1316,16 +1356,16 @@
     tokens_hbm, x_hbm, y_grad_hbm, states_hbm, columns_hbm, gated_hbm, gated_t_hbm, gate_grad_hbm, normed_t_hbm,
     cotangents_hbm, cotangent_hbm, weight_out_hbm, weight_gate_hbm, weight_x_hbm,
     layer_out_hbm, token_grad_hbm, gate_back, x_back, small_back,
-    out_raw_ref, vectors_ref, total_ref,
+    out_raw_ref, vectors_ref, gains_ref, total_ref,
     x_part, y_grad, states, columns, padded, following, state_back, inner_grad,
     x_grad, key_grad, query_grad, sums_ref, rest_ref, channel_ref,
     normed_t, gate_grad, gated_t, cotangent, wide,
     kept, near_out, near_in,
     shared_out, shared_in, raw, small_t, small_n,
-    vector_sum, vector_in, gate_out, x_out, small_out, scalar_out, scalar_in,
+    vector_sum, vector_in, gain_parts, gain_total, gate_out, x_out, small_out, scalar_out, scalar_in,
     first_held, first_arrived, gate_held, gate_arrived, small_held, small_arrived,
     load_sem, scan_sem, chunk_sem, store_sem, local_sem,
-    near_send, near_recv, swap_send, swap_recv, vector_send, vector_recv, return_send, return_recv,
+    near_send, near_recv, swap_send, swap_recv, vector_send, vector_recv, gain_send, gain_recv, return_send, return_recv,
     scalar_send, scalar_recv, ring_send, ring_recv, ring_free, near_free,
 ):
     ring = Ring()
@@ -1335,15 +1375,16 @@
     rows, rows_out, tokens = D // count, width // count, tokens_hbm.shape[0]
     sub, shared, heads = gate_back.shape[1], shared_part_ref.shape[0], HEADS // 4
     precise = partial(jnp.dot, precision=highest, preferred_element_type=f32)
-    out_ring, gate_ring, x_ring, small_ring = (
+    halves = [pl.ds(0, width // 2), pl.ds(width // 2, width // 2)]
+    out_ring, gate_ring, small_ring, *x_rings = (
         RingScatter(ring, held, arrived, ring_send.at[i], ring_recv.at[i])
         for i, (held, arrived) in enumerate(
             [
                 (first_held, first_arrived),
                 (gate_held, gate_arrived),
-                (first_held, first_arrived),
                 (small_held, small_arrived),
             ]
+            + [(first_held.at[:, :, :, at], first_arrived.at[:, :, at]) for at in halves]
         )
     )
 
@@ -1392,12 +1433,7 @@
     normed_load = load(normed_t_hbm, normed_t, 1)
     gate_grad_load = load(gate_grad_hbm, gate_grad, 2)
     out_load = load(weight_out_hbm, wide, 3)
-    for copy in hop_loads(0) + [cotangent_load, normed_load, gate_grad_load, out_load]:
-        copy.start()
-    gated_load(0, 3).start()
-    gated_load(1, 1).start()
-    x_load(0).start()
-    for copy in scan_loads(0):
+    for copy in hop_loads(0) + [cotangent_load]:
         copy.start()
     greet(
         [{"fsdp": partner(k)} for k in (1, 2, 3)]
@@ -1424,8 +1460,12 @@
     def gate_term(owner, way):
         return dot_rows(normed_t[rows_of(owner), :], gate_grad[...])
 
-    def x_term(owner, way):
-        return dot_rows(normed_t[rows_of(owner), :], x_grad[...])
+    def x_term(at):
+        return lambda owner, way: dot_rows(normed_t[rows_of(owner), :], x_grad[:, at])
+
+    def x_hop(hop):
+        for x_ring, at in zip(x_rings, halves):
+            x_ring.start(hop, x_term(at))
 
     def small_term(owner, way):
         return dot_lanes(normed_t[rows_of(owner), :], small_t[...])
@@ -1460,9 +1500,17 @@
         if group + 1 < groups:
             x_load(group + 1).start()
 
+    cotangent_load.wait()
+    normed_load.start()
+    gate_grad_load.start()
+    out_hop(0)
+    out_load.start()
+    gated_load(0, 3).start()
+    gated_load(1, 1).start()
+    x_load(0).start()
+    for copy in scan_loads(0):
+        copy.start()
     scan_backward_start(key_grad, query_grad, sums_ref, inner_grad)
-    cotangent_load.wait()
-    out_hop(0)
     normed_load.wait()
     gate_grad_load.wait()
     gate_ring.start(0, gate_term)
@@ -1476,8 +1524,9 @@
         near_out[1 - i] = added_block(i).astype(bf16)
         near_copy(0, 1 - i).start()
         gated_load(i, (2, 0)[i]).start()
+    out_hop(1)
     scan(0)
-    out_hop(1)
+    gate_ring.start(1, gate_term)
     gated_load(0, 2).wait()
     value = added_block(0)
     near_copy(0, 1).wait_recv()
@@ -1499,10 +1548,12 @@
     gate_tiles = weight_tiles(weight_gate_hbm, wide, 6)
     for copy in gate_tiles:
         copy.start()
+    out_hop(2)
     scan(1)
-    gate_ring.start(1, gate_term)
+    gate_ring.start(2, gate_term)
     scan(2)
-    out_hop(2)
+    for hop in range(3, far):
+        out_hop(hop)
     scan(3)
     scan_backward_finish(key_ref, query_ref, key_grad, query_grad, inner_grad)
 
@@ -1518,9 +1569,24 @@
 
     for k in (2, 3, 1):
         shared_copy(k).start()
+    for copy in hop_loads(far):
+        copy.wait()
+    value = out_ring.finish(out_term(far))
+    out_raw_ref[...] = jnp.concatenate([value[:rows_out], value[rows_out:]], axis=1)
+    squares = total_squares(value)
+    for way in (0, 1):
+        pl.semaphore_signal(
+            ring_free.at[way], inc=1, device_id=ring.target(1 - way), device_id_type=MESH
+        )
+    x_tiles = weight_tiles(weight_x_hbm, cotangent, 10)
+    for copy in x_tiles:
+        copy.start()
+    for way in (0, 1):
+        pl.semaphore_wait(ring_free.at[way], 1)
+    x_hop(0)
+
     for hop in range(3, far):
-        out_hop(hop)
-    gate_ring.start(2, gate_term)
+        gate_ring.start(hop, gate_term)
 
     at_row = lax.broadcasted_iota(jnp.int32, (SPAN, SPAN), 0)
     at_lane = lax.broadcasted_iota(jnp.int32, (SPAN, SPAN), 1)
@@ -1572,6 +1638,39 @@
     small_n[...] = small_t[...].T
     small_ring.start(0, small_term)
 
+    vector_sum[...] = jnp.zeros_like(vector_sum)
+    vector_sum[0:1, :] = gate_gain_ref[0:1, :]
+    vector_sum[1 : CONV + 3, :] = channel_ref[0 : CONV + 2, :]
+    vector_sum[15:16, 0:PAIR] = step_bias_grad
+    vector_sum[15:16, PAIR : 2 * PAIR] = decay_grad
+    across = jnp.concatenate([shared_sums, jnp.zeros((PAIR - shared, PAIR), f32)], axis=0)
+    vector_sum[16:24, 0:PAIR] = across.T[0:8]
+    flips = []
+    while 1 << len(flips) < count:
+        flips.append(1 << len(flips))
+
+    def vector_copy(step):
+        return pltpu.make_async_remote_copy(
+            vector_in.at[step, 0], vector_in.at[step, 1], vector_send.at[step],
+            vector_recv.at[step],
+            device_id={"dp": flipped(d, flips[step])}, device_id_type=MESH,
+        )
+
+    def vector_step(step):
+        if step:
+            vector_copy(step - 1).wait_recv()
+            vector_sum[...] = vector_sum[...] + vector_in[step - 1, 1]
+        if step < len(flips):
+            vector_in[step, 0] = vector_sum[...]
+            vector_copy(step).start()
+
+    def vector_spread(k):
+        return to_partner(
+            k, vector_sum, vectors_ref.at[f], vector_send, vector_recv, len(flips) + k - 1
+        )
+
+    vector_step(0)
+
     near_copy(0, 0).wait_send()
     tokens_load = load(tokens_hbm, near_out.at[0], 15)
     tokens_load.start()
@@ -1590,24 +1689,6 @@
     near_out[2] = value.astype(bf16)
     layer_store = pltpu.make_async_copy(near_out.at[2], layer_out_hbm, store_sem.at[0])
     layer_store.start()
-
-    for copy in hop_loads(far):
-        copy.wait()
-    value = out_ring.finish(out_term(far))
-    out_raw_ref[...] = jnp.concatenate([value[:rows_out], value[rows_out:]], axis=1)
-    squares = total_squares(value)
-    for way in (0, 1):
-        pl.semaphore_signal(
-            ring_free.at[way], inc=1, device_id=ring.target(1 - way), device_id_type=MESH
-        )
-    x_tiles = weight_tiles(weight_x_hbm, cotangent, 10)
-    for copy in x_tiles:
-        copy.start()
-    for way in (0, 1):
-        pl.semaphore_wait(ring_free.at[way], 1)
-    x_ring.start(0, x_term)
-    for hop in range(3, far):
-        gate_ring.start(hop, gate_term)
 
     for copy in gate_tiles + x_tiles:
         copy.wait()
@@ -1629,12 +1710,14 @@
         back_block(flip, near_out.at[i], bf16)
         near_copy(1, i).start()
     small_ring.start(1, small_term)
+    vector_step(1)
     back_block(2, kept, f32)
     near_copy(1, 1).wait_recv()
     layer_store.wait()
     near_out[2] = (kept[...] + near_in[1].astype(f32)).astype(bf16)
     near_copy(1, 2).start()
-    x_ring.start(1, x_term)
+    x_hop(1)
+    vector_step(2)
     back_block(0, kept, f32)
     near_copy(1, 1).wait_send()
     own_load = load(cotangent_hbm, near_out.at[1], 14)
@@ -1643,23 +1726,25 @@
     tokens_load = load(tokens_hbm, near_out.at[0], 15)
     tokens_load.start()
 
+    returned = [(gate_out, gate_back), (small_out, small_back)] + [
+        (x_out.at[:, at], x_back.at[:, :, at]) for at in halves
+    ]
+
     def return_copy(part, k):
-        source = (gate_out, x_out, small_out)[part]
-        target = (gate_back, x_back, small_back)[part]
+        source, target = returned[part]
         return to_partner(
             k, row_slice(source, partner(k) * sub, sub), target.at[f],
             return_send, return_recv, part * 3 + k - 1,
         )
 
     def own_copy(part):
-        source = (gate_out, x_out, small_out)[part]
-        target = (gate_back, x_back, small_back)[part]
+        source, target = returned[part]
         return pltpu.make_async_copy(
             row_slice(source, f * sub, sub), target.at[f], local_sem.at[part]
         )
 
     def give_back(part, value):
-        (gate_out, x_out, small_out)[part][...] = value.astype(bf16)
+        returned[part][0][...] = value.astype(bf16)
         for k in (2, 3, 1):
             return_copy(part, k).start()
         own_copy(part).start()
@@ -1668,7 +1753,11 @@
     squares = squares + total_squares(value)
     give_back(0, value)
     small_ring.start(2, small_term)
-    x_ring.start(2, x_term)
+    x_hop(2)
+    vector_step(3)
+    for k in (2, 3, 1):
+        vector_spread(k).start()
+    vectors_ref[f] = vector_sum[...]
     near_copy(1, 0).wait_recv()
     near_copy(1, 2).wait_recv()
     own_load.wait()
@@ -1686,53 +1775,52 @@
     token_store.start()
     gain_grad = jnp.sum(normed_grad * scaled, axis=0, keepdims=True)
 
-    vector_sum[...] = jnp.zeros_like(vector_sum)
-    vector_sum[0:1, :] = gate_gain_ref[0:1, :]
-    vector_sum[1 : CONV + 3, :] = channel_ref[0 : CONV + 2, :]
-    for i in range(D // width):
-        vector_sum[CONV + 3 + i : CONV + 4 + i, :] = gain_grad[:, i * width : (i + 1) * width]
-    vector_sum[15:16, 0:PAIR] = step_bias_grad
-    vector_sum[15:16, PAIR : 2 * PAIR] = decay_grad
-    across = jnp.concatenate([shared_sums, jnp.zeros((PAIR - shared, PAIR), f32)], axis=0)
-    vector_sum[16:24, 0:PAIR] = across.T[0:8]
-
-    def vector_copy(step, flip):
+    for i in range(8):
+        gain_parts[0, i : i + 1, :] = gain_grad[:, i * (D // 8) : (i + 1) * (D // 8)]
+
+    def over_dp(k, source, target, send, recv, at):
+        member = d
+        for bit in flips:
+            if k & bit:
+                member = flipped(member, bit)
         return pltpu.make_async_remote_copy(
-            vector_in.at[step, 0], vector_in.at[step, 1], vector_send.at[step],
-            vector_recv.at[step],
-            device_id={"dp": flipped(d, flip)}, device_id_type=MESH,
-        )
-
-    flips = []
-    while 1 << len(flips) < count:
-        flips.append(1 << len(flips))
-    for step, flip in enumerate(flips):
-        vector_in[step, 0] = vector_sum[...]
-        vector_copy(step, flip).start()
-        if step == 0:
-            for hop in range(3, far):
-                small_ring.start(hop, small_term)
-        if step == 1:
-            for hop in range(3, far):
-                x_ring.start(hop, x_term)
-        vector_copy(step, flip).wait_recv()
-        vector_sum[...] = vector_sum[...] + vector_in[step, 1]
-
-    def vector_spread(k):
+            source, target, send.at[at], recv.at[at],
+            device_id={"dp": member}, device_id_type=MESH,
+        )
+
+    def gain_copy(k):
+        return over_dp(k, gain_parts.at[0], gain_parts.at[k], gain_send, gain_recv, k)
+
+    def paired(parts):
+        while len(parts) > 1:
+            parts = [parts[i] + parts[i + 1] for i in range(0, len(parts), 2)]
+        return parts[0]
+
+    for k in range(count - 1, 0, -1):
+        gain_copy(k).start()
+    for hop in range(3, far):
+        small_ring.start(hop, small_term)
+        x_hop(hop)
+    for k in range(1, count):
+        gain_copy(k).wait_recv()
+    gain_total[...] = paired([gain_parts[k] for k in range(count)])
+
+    def gain_spread(k):
         return to_partner(
-            k, vector_sum, vectors_ref.at[f], vector_send, vector_recv, len(flips) + k - 1
+            k, gain_total, gains_ref.at[f], gain_send, gain_recv, count + k - 1
         )
 
     for k in (2, 3, 1):
-        vector_spread(k).start()
-    vectors_ref[f] = vector_sum[...]
+        gain_spread(k).start()
+    gains_ref[f] = gain_total[...]
 
     value = small_ring.finish(small_term)
     squares = squares + total_squares(value)
-    give_back(2, value)
-    value = x_ring.finish(x_term)
     give_back(1, value)
-    squares = squares + total_squares(value)
+    for part, (x_ring, at) in enumerate(zip(x_rings, halves)):
+        value = x_ring.finish(x_term(at))
+        give_back(2 + part, value)
+        squares = squares + total_squares(value)
 
     total = jnp.broadcast_to(squares, (8, PAIR))
     scalar_out[0] = total
@@ -1750,13 +1838,8 @@
     scalar_out[1] = total
 
     def far_scalar(k):
-        member = d
-        for bit in flips:
-            if k & bit:
-                member = flipped(member, bit)
-        return pltpu.make_async_remote_copy(
-            scalar_out.at[1], scalar_in.at[3 + k], scalar_send.at[3 + k], scalar_recv.at[3 + k],
-            device_id={"dp": member}, device_id_type=MESH,
+        return over_dp(
+            k, scalar_out.at[1], scalar_in.at[3 + k], scalar_send, scalar_recv, 3 + k
         )
 
     for k in range(count - 1, 0, -1):
@@ -1765,25 +1848,26 @@
     for k in range(1, count):
         far_scalar(k).wait_recv()
         parts.append(scalar_in[3 + k])
-    while len(parts) > 1:
-        parts = [parts[i] + parts[i + 1] for i in range(0, len(parts), 2)]
-    total_ref[...] = parts[0]
+    total_ref[...] = paired(parts)
 
     for k in (1, 2, 3):
         vector_spread(k).wait_recv()
         vector_spread(k).wait_send()
+        gain_spread(k).wait_recv()
+        gain_spread(k).wait_send()
         shared_copy(k).wait_send()
         near_scalar(k).wait_send()
-        for i in range(3):
+        for i in range(4):
             return_copy(i, k).wait_recv()
             return_copy(i, k).wait_send()
     for k in range(1, count):
         far_scalar(k).wait_send()
+        gain_copy(k).wait_send()
     near_copy(1, 2).wait_send()
-    for i in range(3):
+    for i in range(4):
         own_copy(i).wait()
-    for step, flip in enumerate(flips):
-        vector_copy(step, flip).wait_send()
+    for step in range(len(flips)):
+        vector_copy(step).wait_send()
     token_store.wait()
 
 
@@ -1808,7 +1892,7 @@
     return pl.pallas_call(
         backward_kernel,
         in_specs=[whole_spec()] * 16 + any_specs(14),
-        out_specs=any_specs(5) + [whole_spec()] * 3,
+        out_specs=any_specs(5) + [whole_spec()] * 4,
         out_shape=[
             sd((own, D), bf16),
             sd((own, D), bf16),
@@ -1817,6 +1901,7 @@
             sd((members, sub, PAIR), bf16),
             sd((rows_out, D), f32),
             sd((members, 24, width), f32),
+            sd((members, 8, D // 8), f32),
             sd((8, PAIR), f32),
         ],
         scratch_shapes=[
@@ -1849,6 +1934,8 @@
             vmem((length, PAIR), bf16),
             vmem((24, width), f32),
             vmem((hops, 2, 24, width), f32),
+            vmem((count, 8, D // 8), f32),
+            vmem((8, D // 8), f32),
             vmem((rows, width), bf16),
             vmem((rows, width), bf16),
             vmem((rows, PAIR), bf16),
@@ -1862,24 +1949,26 @@
             dma((3, 3)),
             dma((4,)),
             dma((2,)),
-            dma((3,)),
+            dma((4,)),
             dma((6,)),
             dma((6,)),
             dma((3,)),
             dma((3,)),
             dma((hops + 3,)),
             dma((hops + 3,)),
-            dma((9,)),
-            dma((9,)),
+            dma((count + 3,)),
+            dma((count + 3,)),
+            dma((12,)),
+            dma((12,)),
             dma((3 + count,)),
             dma((3 + count,)),
-            dma((4, 2 * far)),
-            dma((4, 2 * far)),
+            dma((5, 2 * far)),
+            dma((5, 2 * far)),
             pltpu.SemaphoreType.REGULAR((2,)),
             pltpu.SemaphoreType.REGULAR((2,)),
         ],
         compiler_params=pltpu.CompilerParams(
-            collective_id=1, has_side_effects=True, vmem_limit_bytes=BACKWARD_VMEM_BYTES
+            collective_id=1, has_side_effects=True, vmem_limit_bytes=VMEM_BYTES
         ),
         name="backward",
     )(
@@ -1894,28 +1983,31 @@
 
 
 def optimizer_kernel(
-    squares_ref, parts_ref, vector_ref, vector_first_ref, vector_second_ref, turn_ref,
+    squares_ref, parts_ref, gains_ref, vector_ref, vector_first_ref, vector_second_ref, turn_ref,
     gate_ref, x_ref, small_ref, in_ref, in_first_ref, in_second_ref,
-    out_raw_ref, out_ref, out_first_ref, out_second_ref,
+    out_raw_ref, out_ref, out_first_ref, out_second_ref, layer_ref, token_ref,
     norm_ref, vector_grad_ref, vector_moment_ref, vector_square_ref, vector_master_ref,
     in_grad_ref, in_moment_ref, in_square_ref, in_master_ref, in_rounded_ref,
     out_grad_ref, out_moment_ref, out_square_ref, out_master_ref, out_rounded_ref,
+    layer_out_ref, token_out_ref,
     joined, factor_ref, in_raw,
 ):
     members = parts_ref.shape[0]
     pairs = INNER // PAIR
     shared, heads = 2 * STATE // members, HEADS // members
+    layer_out_ref[...] = layer_ref[...]
+    token_out_ref[...] = token_ref[...]
 
     @pl.when(pl.program_id(0) == 0)
     def _():
         joined[...] = jnp.zeros_like(joined)
         width = parts_ref.shape[2]
         for i in range(D // PAIR):
-            row = CONV + 3 + i * PAIR // width
-            lanes = slice(i * PAIR % width, i * PAIR % width + PAIR)
-            value = parts_ref[0, row : row + 1, lanes]
+            row = i * PAIR // (D // 8)
+            lanes = slice(i * PAIR % (D // 8), i * PAIR % (D // 8) + PAIR)
+            value = gains_ref[0, row : row + 1, lanes]
             for member in range(1, members):
-                value = value + parts_ref[member, row : row + 1, lanes]
+                value = value + gains_ref[member, row : row + 1, lanes]
             joined[i : i + 1, :] = value
 
         def put_channels(first_row, row):
@@ -1959,7 +2051,7 @@
         joined[LAST_ROW + 1 : LAST_ROW + 2, :] = skips
         vector_raw = joined[...]
         norm = jnp.sqrt(squares_ref[...] + total_squares(vector_raw))
-        norm_ref[...] = norm
+        norm_ref[0, 0] = norm[0, 0]
         factor = jnp.minimum(1.0, clip_norm / (norm + 1e-06))
         factor_ref[...] = factor
         grad = vector_raw * factor[0:1, 0:1]
@@ -1994,7 +2086,7 @@
     out_rounded_ref[...] = master.astype(bf16)
 
 
-def optimizer(squares, parts, vectors, gate, x, small, in_state, out_raw, out_state):
+def optimizer(squares, parts, gains, vectors, gate, x, small, in_state, out_raw, out_state, passed):
     members, rows, width = x.shape
     in_shape, out_shape = in_state[0].shape, out_state[0].shape
     steps = OPTIMIZER_STEPS
@@ -2002,22 +2094,29 @@
     piece = lambda lanes: pl.BlockSpec((members, step_rows, lanes), lambda i: (0, i, 0))
     in_flat = pl.BlockSpec((step_rows, in_shape[1]), lambda i: (i, 0))
     out_flat = pl.BlockSpec((out_shape[0] // steps, out_shape[1]), lambda i: (i, 0))
+    row_flat = pl.BlockSpec((passed[0].shape[0] // steps, D), lambda i: (i, 0))
     sd = jax.ShapeDtypeStruct
     vector_shape = sd(vectors[0].shape, f32)
     return pl.pallas_call(
         optimizer_kernel,
         grid=(steps,),
-        in_specs=[whole_spec()] * 6
+        in_specs=[whole_spec()] * 7
         + [piece(width), piece(width), piece(PAIR)]
         + [in_flat] * 3
-        + [out_flat] * 4,
-        out_specs=[whole_spec()] * 5 + [in_flat] * 5 + [out_flat] * 5,
-        out_shape=[sd((8, PAIR), f32)]
+        + [out_flat] * 4
+        + [row_flat] * 2,
+        out_specs=[pl.BlockSpec(memory_space=pltpu.SMEM)]
+        + [whole_spec()] * 4
+        + [in_flat] * 5
+        + [out_flat] * 5
+        + [row_flat] * 2,
+        out_shape=[sd((1, 1), f32)]
         + [vector_shape] * 4
         + [sd(in_shape, f32)] * 4
         + [sd(in_shape, bf16)]
         + [sd(out_shape, f32)] * 4
-        + [sd(out_shape, bf16)],
+        + [sd(out_shape, bf16)]
+        + [sd(v.shape, v.dtype) for v in passed],
         scratch_shapes=[
             pltpu.VMEM(vectors[0].shape, f32),
             pltpu.VMEM((8, PAIR), f32),
@@ -2026,8 +2125,8 @@
         compiler_params=pltpu.CompilerParams(vmem_limit_bytes=VMEM_BYTES),
         name="optimizer",
     )(
-        squares, parts, *vectors, last_columns(members), gate, x, small, *in_state, out_raw,
-        *out_state,
+        squares, parts, gains, *vectors, last_columns(members), gate, x, small, *in_state, out_raw,
+        *out_state, *passed,
     )
 
 
@@ -2218,19 +2317,22 @@
 
     if in_kernels:
         (
-            layer_out, token_grad, gate_back, x_back, small_back, out_raw, vector_rows, squares,
+            layer_out, token_grad, gate_back, x_back, small_back, out_raw, vector_rows, gains,
+            squares,
         ) = backward(
             scan_inputs, queries_t, head_all, head_consts, shared_part, shared_pre, shared_taps,
             vector_state[0], gain_grad, tokens, weight_shared, x_part, y_grad, states, gated_low,
             gated_t, gate_grad, normed_t, cotangents, cotangent, weight_out, weight_gate, weight_x,
         )
         norm, *rest = optimizer(
-            squares, vector_rows, vector_state, gate_back, x_back, small_back,
+            squares, vector_rows, gains, vector_state, gate_back, x_back, small_back,
             (in_weight, in_first, in_second), out_raw, (out_weight, out_first, out_second),
+            (layer_out, token_grad),
         )
         vector_out = [v.reshape(-1)[: vectors.shape[0]] for v in rest[:4]]
         in_grad, in_moment, in_square, in_master, in_rounded = rest[4:9]
-        out_grad, out_moment, out_square, out_master, out_rounded = rest[9:]
+        out_grad, out_moment, out_square, out_master, out_rounded = rest[9:14]
+        layer_out, token_grad = rest[14:]
         return (
             layer_out,
             token_grad,

time: 358 us -> 344 us (0.961)
  Pallas kernels: 347 us -> 337 us
    pallas_call x1, Pallas kernels: 176 us -> 169 us  [forward(): pl.pallas_call(forward_kernel, in_specs=[whole_spec()] + any_specs(1) + [...]
    pallas_call x1, Pallas kernels: 158 us -> 154 us  [backward(): pl.pallas_call(backward_kernel, in_specs=[whole_spec()] * 16 + any_specs(...]
where the time goes in v1:
time: 344 us; the launch traced here: 342 us
  Pallas kernels  337 us (98%)
    pallas_call x1, Pallas kernels, forward(): pl.pallas_call(forward_kernel, in_specs=[whole_spec()] + any_specs(1) + [...  169 us
    pallas_call x1, Pallas kernels, backward(): pl.pallas_call(backward_kernel, in_specs=[whole_spec()] * 16 + any_specs(...  154 us
    pallas_call x1, Pallas kernels, optimizer(): pl.pallas_call(optimizer_kernel, grid=(steps,), in_specs=[whole_spec()] *...  14 us

profile of v1, /device:TPU:0, one launch (start us, length us, event | category | flops | bytes accessed | tf_op | source)
XLA Modules:
  0.0 341.6 jit_solution(6427826021383629771)
XLA Ops:
  0.7 1.6 pad_bitcast_fusion.2.vectors_ref.vectors_own_ref.vector_ref
  2.9 0.6 broadcast_in_dim.3.active_ref
  3.5 169.1 %forward.1 = (bf16[2048,128]{1,0:T(8,128)(2,1)}, bf16[2048,1024]{1,0:T(8,128)(2,1)}, bf16[2048,1024]{1,0:T(8,128)(2,1)}, bf16[1024,2048]{1,0:T(8,128)(2,1)}, bf1...) custom-call(bf16[256,2048]{1,0:T(8,128)(2,1)} %tokens_hbm.1, ...), custom_call_target="tpu_custom_call" | custom-call | tf_op jit(solution)/shard_map/forward/pallas_call | solution.py:1250
  172.5 0.0 copy-start
  172.5 0.0 copy-start.1
  172.5 154.1 %backward.1 = (bf16[256,2048]{1,0:T(8,128)(2,1)}, bf16[256,2048]{1,0:T(8,128)(2,1)}, bf16[4,64,1024]{2,1,0:T(8,128)(2,1)}, bf16[4,64,1024]{2,1,0:T(8,128)(2,1)},...) custom-call(f32[32,1024]{1,0:T(8,128)} %get-tuple-element.67.rows_re, ...), custom_call_target="tpu_custom_call" | custom-call | tf_op jit(solution)/shard_map/backward/pallas_call | solution.py:1892
  326.6 0.0 copy-done
  326.7 0.0 copy-done.1
  326.7 0.7 pad_bitcast_fusion
  327.4 14.0 %optimizer.1 = (f32[1,1]{1,0:T(1,128)}, f32[220,128]{1,0:T(8,128)}, f32[220,128]{1,0:T(8,128)}, f32[220,128]{1,0:T(8,128)}, f32[220,128]{1,0:T(8,128)}, /*index=...) custom-call(f32[8,128]{1,0:T(8,128)} %get-tuple-element.91.squares_r, ...), custom_call_target="tpu_custom_call" | custom-call | tf_op jit(solution)/shard_map/optimizer/pallas_call | solution.py:2100
Async XLA Ops:
  172.5 154.1 %copy-start = (f32[28096]{0:T(1024)S(1)}, f32[28096]{0:T(1024)}, u32[]{:S(2)}) copy-start(f32[28096]{0:T(1024)} %param.29) | copy-start | bytes 337156
  172.5 154.1 %copy-start.1 = (f32[28096]{0:T(1024)S(1)}, f32[28096]{0:T(1024)}, u32[]{:S(2)}) copy-start(f32[28096]{0:T(1024)} %param.28) | copy-start | bytes 337156

commit v2 on v1

--- a/solution.py
+++ b/solution.py
@@ -1552,6 +1552,26 @@
     scan(1)
     gate_ring.start(2, gate_term)
     scan(2)
+
+    near_copy(0, 0).wait_send()
+    tokens_load = load(tokens_hbm, near_out.at[0], 15)
+    tokens_load.start()
+    near_copy(0, 0).wait_recv()
+    near_copy(0, 2).wait_recv()
+    tokens_load.wait()
+    value = near_out[0].astype(f32) + (
+        (kept[...] + near_in[0].astype(f32)) + near_in[2].astype(f32)
+    )
+    for k in (0, 1):
+        pl.semaphore_signal(
+            near_free.at[k], inc=1, device_id={"fsdp": partner(k + 1)}, device_id_type=MESH
+        )
+    for i in (1, 2):
+        near_copy(0, i).wait_send()
+    near_out[2] = value.astype(bf16)
+    layer_store = pltpu.make_async_copy(near_out.at[2], layer_out_hbm, store_sem.at[0])
+    layer_store.start()
+
     for hop in range(3, far):
         out_hop(hop)
     scan(3)
@@ -1671,25 +1691,6 @@
 
     vector_step(0)
 
-    near_copy(0, 0).wait_send()
-    tokens_load = load(tokens_hbm, near_out.at[0], 15)
-    tokens_load.start()
-    near_copy(0, 0).wait_recv()
-    near_copy(0, 2).wait_recv()
-    tokens_load.wait()
-    value = near_out[0].astype(f32) + (
-        (kept[...] + near_in[0].astype(f32)) + near_in[2].astype(f32)
-    )
-    for k in (0, 1):
-        pl.semaphore_signal(
-            near_free.at[k], inc=1, device_id={"fsdp": partner(k + 1)}, device_id_type=MESH
-        )
-    for i in (1, 2):
-        near_copy(0, i).wait_send()
-    near_out[2] = value.astype(bf16)
-    layer_store = pltpu.make_async_copy(near_out.at[2], layer_out_hbm, store_sem.at[0])
-    layer_store.start()
-
     for copy in gate_tiles + x_tiles:
         copy.wait()
 
@@ -1706,16 +1707,17 @@
 
     for k in (0, 1):
         pl.semaphore_wait(near_free.at[k], 1)
-    for i, flip in ((1, 3), (0, 1)):
-        back_block(flip, near_out.at[i], bf16)
-        near_copy(1, i).start()
-    small_ring.start(1, small_term)
-    vector_step(1)
+    back_block(3, near_out.at[1], bf16)
+    near_copy(1, 1).start()
     back_block(2, kept, f32)
     near_copy(1, 1).wait_recv()
     layer_store.wait()
     near_out[2] = (kept[...] + near_in[1].astype(f32)).astype(bf16)
     near_copy(1, 2).start()
+    small_ring.start(1, small_term)
+    vector_step(1)
+    back_block(1, near_out.at[0], bf16)
+    near_copy(1, 0).start()
     x_hop(1)
     vector_step(2)
     back_block(0, kept, f32)

time: 344 us -> 344 us (level)
  no operation moved by 1% of the time
where the time goes in v2:
time: 344 us; the launch traced here: 342 us
  Pallas kernels  337 us (98%)
    pallas_call x1, Pallas kernels, forward(): pl.pallas_call(forward_kernel, in_specs=[whole_spec()] + any_specs(1) + [...  170 us
    pallas_call x1, Pallas kernels, backward(): pl.pallas_call(backward_kernel, in_specs=[whole_spec()] * 16 + any_specs(...  154 us
    pallas_call x1, Pallas kernels, optimizer(): pl.pallas_call(optimizer_kernel, grid=(steps,), in_specs=[whole_spec()] *...  14 us

profile of v2, /device:TPU:0, one launch (start us, length us, event | category | flops | bytes accessed | tf_op | source)
XLA Modules:
  0.0 342.2 jit_solution(10836823660340062448)
XLA Ops:
  0.7 1.6 pad_bitcast_fusion.2.vectors_ref.vectors_own_ref.vector_ref
  2.9 0.6 broadcast_in_dim.3.active_ref
  3.5 169.8 %forward.1 = (bf16[2048,128]{1,0:T(8,128)(2,1)}, bf16[2048,1024]{1,0:T(8,128)(2,1)}, bf16[2048,1024]{1,0:T(8,128)(2,1)}, bf16[1024,2048]{1,0:T(8,128)(2,1)}, bf1...) custom-call(bf16[256,2048]{1,0:T(8,128)(2,1)} %tokens_hbm.1, ...), custom_call_target="tpu_custom_call" | custom-call | tf_op jit(solution)/shard_map/forward/pallas_call | solution.py:1250
  173.2 0.0 copy-start
  173.3 0.0 copy-start.1
  173.3 153.7 %backward.1 = (bf16[256,2048]{1,0:T(8,128)(2,1)}, bf16[256,2048]{1,0:T(8,128)(2,1)}, bf16[4,64,1024]{2,1,0:T(8,128)(2,1)}, bf16[4,64,1024]{2,1,0:T(8,128)(2,1)},...) custom-call(f32[32,1024]{1,0:T(8,128)} %get-tuple-element.67.rows_re, ...), custom_call_target="tpu_custom_call" | custom-call | tf_op jit(solution)/shard_map/backward/pallas_call | solution.py:1894
  327.0 0.0 copy-done
  327.0 0.0 copy-done.1
  327.0 0.9 pad_bitcast_fusion
  327.9 14.0 %optimizer.1 = (f32[1,1]{1,0:T(1,128)}, f32[220,128]{1,0:T(8,128)}, f32[220,128]{1,0:T(8,128)}, f32[220,128]{1,0:T(8,128)}, f32[220,128]{1,0:T(8,128)}, /*index=...) custom-call(f32[8,128]{1,0:T(8,128)} %get-tuple-element.91.squares_r, ...), custom_call_target="tpu_custom_call" | custom-call | tf_op jit(solution)/shard_map/optimizer/pallas_call | solution.py:2102
Async XLA Ops:
  173.2 153.7 %copy-start = (f32[28096]{0:T(1024)S(1)}, f32[28096]{0:T(1024)}, u32[]{:S(2)}) copy-start(f32[28096]{0:T(1024)} %param.29) | copy-start | bytes 337156
  173.3 153.7 %copy-start.1 = (f32[28096]{0:T(1024)S(1)}, f32[28096]{0:T(1024)}, u32[]{:S(2)}) copy-start(f32[28096]{0:T(1024)} %param.28) | copy-start | bytes 337156
